TPU v7x, 128 devices: a whole 4x4x4 slice. The times are simulated.
128 devices in a mesh: sec: 4 (over z), space: 32 (over x, y, core).
Axes of the slice: x: 4, y: 4, z: 4, core: 2. Of those that a mesh axis runs over, the one named last changes fastest.
Arguments:
- grid_feat: bfloat16 [4, 32768, 1024], P('sec', 'space'), may hold values from -12 to 12
- mesh_feat: bfloat16 [4, 16384, 1024], P('sec', 'space'), may hold values from -27 to 27
- mesh_adjoint: bfloat16 [4, 16384, 1024], P('sec', 'space'), may hold values from -6 to 6
- w_query: bfloat16 [1024, 1024], replicated, may hold values from -1 to 1
- w_key: bfloat16 [1024, 1024], replicated, may hold values from -1 to 1
- w_value: bfloat16 [1024, 1024], replicated, may hold values from -0.1875 to 0.1875
- block_grid: int32 [512], P('space'), may hold values from 0 to 255, as said below
- block_mask: int32 [512, 128, 128], P('space'), may hold values from 0 to 1, as said below
Outputs:
- grid_grad: bfloat16 [4, 32768, 1024], P('sec', 'space')
- mesh_grad: bfloat16 [4, 16384, 1024], P('sec', 'space')
- w_grad: float32 [1024, 3072], P(('sec', 'space'))
Inputs may be any that keep to these rules, and one draw needn't show every extreme that they name: `block_grid`: each mesh block of a band has 4 consecutive slots listing distinct grid blocks of its own band or the nearest block of an adjacent band; the first is the own band's block number m * 2 within the band for mesh block m; where the band below exists, the band's first mesh block lists its nearest block in the second slot; where the band above exists, the band's last mesh block lists its nearest block in the second slot. `block_mask`: the first slot of each mesh block holds the diagonal, so every mesh node has an edge; in each band, the last slots of every mesh block (the same number for all of its mesh blocks, at least min(3, 4) slots live) may be all zeros; band 0 has none such.
All inputs are finite; a program needn't handle non-finite values.
Results may differ from a plain program's by a relative error of at most 0.015.
The roundings to bfloat16 on the way count: a program that leaves them out, or rounds other values in their place, can miss the bound.
Values may be sent and summed in bfloat16 or wider, within the bound.
A program may use at most 128 MiB of HBM per device.

v0:
```python
import jax
import jax.numpy as jnp
from jax import lax
from jax.sharding import PartitionSpec as P

DH = 64
BLOCK = 128
K = 4


def passed_along(value, axis, steps):
    count = lax.axis_size(axis)
    pairs = [(source, (source + steps) % count) for source in range(count)]
    return lax.ppermute(value, axis, pairs)


def with_halo(shard, sides, width):
    for axis, dim in sides:
        devices, length = (lax.axis_size(axis), shard.shape[dim])
        up = [(i, (i + 1) % devices) for i in range(devices - 1)]
        down = [(j, i) for i, j in up]
        last = lax.slice_in_dim(shard, length - width, length, axis=dim)
        initial = lax.slice_in_dim(shard, 0, width, axis=dim)
        before = lax.ppermute(last, axis, up)
        after = lax.ppermute(initial, axis, down)
        shard = jnp.concatenate([before, shard, after], axis=dim)
    return shard


def passed_along_2(shard, axis, by):
    devices = lax.axis_size(axis)
    pairs = [(i, i + by) for i in range(devices) if 0 <= i + by < devices]
    return lax.ppermute(shard, axis, pairs)


def times_transposed(left, weight):
    return lax.dot_general(
        left, weight, (((1,), (1,)), ((), ())), preferred_element_type=jnp.float32
    )


def attend(query_blk, adjoint_blk, kv_rows, masks):
    rows = query_blk.shape[0]
    width = query_blk.shape[1]
    heads = width // DH
    scale = DH ** (-0.5)
    query_h = query_blk.reshape(rows, heads, DH)
    keys = kv_rows[:, :width].reshape(-1, heads, DH)
    values = kv_rows[:, width:].reshape(-1, heads, DH)
    live = masks.transpose(1, 0, 2).reshape(rows, -1) > 0
    scores = jnp.einsum("rhd,chd->hrc", query_h, keys, preferred_element_type=jnp.float32) * scale
    shifted = jnp.where(live[None], scores, -1e30)
    top = jnp.max(shifted, axis=-1, keepdims=True)
    expo = jnp.where(live[None], jnp.exp(shifted - top), 0.0)
    probs = expo / jnp.sum(expo, axis=-1, keepdims=True)
    probs_b = probs.astype(jnp.bfloat16)
    attended = jnp.einsum("hrc,chd->rhd", probs_b, values, preferred_element_type=jnp.float32)
    adjoint_h = adjoint_blk.reshape(rows, heads, DH)
    delta = jnp.sum(adjoint_h.astype(jnp.float32) * attended, axis=-1).T[:, :, None]
    dprobs = jnp.einsum("rhd,chd->hrc", adjoint_h, values, preferred_element_type=jnp.float32)
    dscores = (probs * (dprobs - delta) * scale).astype(jnp.bfloat16)
    dquery = jnp.einsum("hrc,chd->rhd", dscores, keys, preferred_element_type=jnp.float32).reshape(
        rows, width
    )
    dkey = jnp.einsum("hrc,rhd->chd", dscores, query_h, preferred_element_type=jnp.float32).reshape(
        -1, width
    )
    dvalue = jnp.einsum(
        "hrc,rhd->chd", probs_b, adjoint_h, preferred_element_type=jnp.float32
    ).reshape(-1, width)
    return (dquery, jnp.concatenate([dkey, dvalue], axis=1))


def on_device(grid_feat, mesh_feat, mesh_adjoint, w_query, w_key, w_value, block_grid, block_mask):
    arrived = passed_along(mesh_adjoint, "sec", -1)[0]
    feats = grid_feat[0]
    nodes = mesh_feat[0]
    width = feats.shape[1]
    grid_blocks = feats.shape[0] // BLOCK
    mesh_blocks = nodes.shape[0] // BLOCK
    band = lax.axis_index("space")
    sections = lax.axis_size("sec")
    w_both = jnp.concatenate([w_key, w_value], axis=1)
    queries = jnp.dot(nodes, w_query, preferred_element_type=jnp.float32).astype(jnp.bfloat16)
    own_kv = jnp.dot(feats, w_both, preferred_element_type=jnp.float32).astype(jnp.bfloat16)
    padded = with_halo(own_kv, (("space", 0),), BLOCK)
    kv_blocks = padded.reshape(grid_blocks + 2, BLOCK, 2 * width)
    local_ids = block_grid - band * grid_blocks + 1

    def step(acc, index):
        start = index * K
        ids = lax.dynamic_slice_in_dim(local_ids, start, K)
        masks = lax.dynamic_slice_in_dim(block_mask, start, K, 0)
        query_blk = lax.dynamic_slice_in_dim(queries, index * BLOCK, BLOCK, 0)
        adjoint_blk = lax.dynamic_slice_in_dim(arrived, index * BLOCK, BLOCK, 0)
        kv_rows = kv_blocks[ids].reshape(K * BLOCK, 2 * width)
        dquery, dkv = attend(query_blk, adjoint_blk, kv_rows, masks)
        acc = acc.at[ids].add(dkv.reshape(K, BLOCK, 2 * width))
        return (acc, dquery)

    start_acc = jnp.zeros((grid_blocks + 2, BLOCK, 2 * width), jnp.float32)
    acc, dqueries = lax.scan(step, start_acc, jnp.arange(mesh_blocks, dtype=jnp.int32))
    acc = acc.reshape(-1, 2 * width)
    from_above = passed_along_2(acc[:BLOCK].astype(jnp.bfloat16), "space", -1).astype(jnp.float32)
    from_below = passed_along_2(acc[-BLOCK:].astype(jnp.bfloat16), "space", 1).astype(jnp.float32)
    core = acc[BLOCK:-BLOCK]
    core = core.at[-BLOCK:].add(from_above)
    core = core.at[:BLOCK].add(from_below)
    dkv_b = core.astype(jnp.bfloat16)
    dquery_b = dqueries.reshape(-1, width).astype(jnp.bfloat16)
    grid_grad = (
        times_transposed(dkv_b[:, :width], w_key) + times_transposed(dkv_b[:, width:], w_value)
    ).astype(jnp.bfloat16)
    mesh_grad = times_transposed(dquery_b, w_query).astype(jnp.bfloat16)
    mesh_term = lax.dot_general(
        nodes, dquery_b, (((0,), (0,)), ((), ())), preferred_element_type=jnp.float32
    )
    grid_term = lax.dot_general(
        feats, dkv_b, (((0,), (0,)), ((), ())), preferred_element_type=jnp.float32
    )
    terms = jnp.concatenate([mesh_term, grid_term], axis=1) / sections
    w_grad = lax.psum_scatter(terms, ("sec", "space"), scatter_dimension=0, tiled=True)
    return (grid_grad[None], mesh_grad[None], w_grad)


def solution(mesh):
    placed = (
        P("sec", "space", None),
        P("sec", "space", None),
        P("sec", "space", None),
        P(),
        P(),
        P(),
        P("space"),
        P("space", None, None),
    )
    return jax.shard_map(
        on_device,
        mesh=mesh,
        in_specs=placed,
        out_specs=(P("sec", "space", None), P("sec", "space", None), P(("sec", "space"), None)),
        check_vma=False,
    )
```

profile of v0, /device:TPU:0, one launch (start us, length us, event | category | flops | bytes accessed | tf_op | source)
XLA Modules:
  0.0 574.6 jit_solution(8173406344458873147)
XLA Ops:
  7.2 2.4 copy.32
  9.6 4.1 collective-permute-start.2
  13.8 6.9 %convert_bitcast_fusion = bf16[1024,2048]{1,0:T(8,128)(2,1)S(1)} fusion(bf16[1024,1024]{1,0:T(8,128)(2,1)} %param.19, bf16[1024,1024]{1,0:T(8,128)(2,1)} %param.18, bf16[1,1024,1024]{2,1,0:T(8,128)(2,1)S(1)} %copy-done), kind=kOutput, calls=%fused_computation.36 | convolution fusion | flops 4305453056 | bytes 10485760 | tf_op jit(solution)/shard_map/dot_general | solution.py:85
  27.6 4.3 convolution_convert_fusion.1
  31.9 4.1 pad_maximum_fusion.1
  36.5 5.3 broadcast_in_dim.43
  41.8 235.5 %while.14 = (s32[]{:T(128)}, f32[10,128,2048]{2,1,0:T(8,128)}, bf16[4,128,1024]{2,1,0:T(8,128)(2,1)}, s32[4]{0:T(128)S(1)}, s32[16]{0:T(128)S(1)}, /*index=5*/bf...) while((s32[]{:T(128)}, f32[10,128,2048]{2,1,0:T(8,128)}, ...), condition=%wide.region_5.6_spmd, body=%wide.region_0.5_spmd.sunk | while | flops 820444672 | bytes 102412744 | solution.py:102
  46.9 4.5 gather_fusion
  51.4 3.0 fusion.87
  58.2 4.7 fusion.88
  62.9 2.6 fusion.89
  68.2 2.9 concatenate.26
  71.1 2.9 copy.61
  74.0 3.6 multiply_convert_fusion.2
  80.3 2.9 concatenate.27
  83.2 2.9 copy.63
  86.1 4.7 pad_maximum_fusion.3
  91.6 9.0 %scatter_fusion = f32[10,128,2048]{2,1,0:T(8,128)} fusion(f32[10,128,2048]{2,1,0:T(8,128)} %get-tuple-element.218, s32[4]{0:T(128)S(1)} %compare_select_fusion.2, f32[4,128,2048]{2,1,0:T(8,128)} %pad_maximum_fusion.3), kind=kCustom, calls=%fused_computation.1.clone.1 | custom fusion | flops 1048576 | bytes 12582928 | tf_op jit(solution)/shard_map/while/body/eval_jaxpr/scatter-add | solution.py:98
  105.7 4.5 gather_fusion
  110.2 3.0 fusion.87
  117.1 4.7 fusion.88
  121.8 2.6 fusion.89
  127.1 2.9 concatenate.26
  130.0 2.9 copy.61
  132.9 3.6 multiply_convert_fusion.2
  139.1 2.9 concatenate.27
  142.0 2.9 copy.63
  144.9 4.7 pad_maximum_fusion.3
  150.5 9.1 %scatter_fusion = f32[10,128,2048]{2,1,0:T(8,128)} fusion(f32[10,128,2048]{2,1,0:T(8,128)} %get-tuple-element.218, s32[4]{0:T(128)S(1)} %compare_select_fusion.2, f32[4,128,2048]{2,1,0:T(8,128)} %pad_maximum_fusion.3), kind=kCustom, calls=%fused_computation.1.clone.1 | custom fusion | flops 1048576 | bytes 12582928 | tf_op jit(solution)/shard_map/while/body/eval_jaxpr/scatter-add | solution.py:98
  164.6 4.5 gather_fusion
  169.1 3.0 fusion.87
  176.0 4.7 fusion.88
  180.7 2.6 fusion.89
  186.0 2.9 concatenate.26
  188.9 2.9 copy.61
  191.8 3.6 multiply_convert_fusion.2
  198.0 2.9 concatenate.27
  200.9 2.9 copy.63
  203.8 4.7 pad_maximum_fusion.3
  209.4 9.1 %scatter_fusion = f32[10,128,2048]{2,1,0:T(8,128)} fusion(f32[10,128,2048]{2,1,0:T(8,128)} %get-tuple-element.218, s32[4]{0:T(128)S(1)} %compare_select_fusion.2, f32[4,128,2048]{2,1,0:T(8,128)} %pad_maximum_fusion.3), kind=kCustom, calls=%fused_computation.1.clone.1 | custom fusion | flops 1048576 | bytes 12582928 | tf_op jit(solution)/shard_map/while/body/eval_jaxpr/scatter-add | solution.py:98
  223.5 4.5 gather_fusion
  228.0 3.0 fusion.87
  234.9 4.7 fusion.88
  239.6 2.6 fusion.89
  244.9 2.9 concatenate.26
  247.8 2.9 copy.61
  250.7 3.6 multiply_convert_fusion.2
  256.9 2.9 concatenate.27
  259.8 2.9 copy.63
  262.7 4.7 pad_maximum_fusion.3
  268.3 9.1 %scatter_fusion = f32[10,128,2048]{2,1,0:T(8,128)} fusion(f32[10,128,2048]{2,1,0:T(8,128)} %get-tuple-element.218, s32[4]{0:T(128)S(1)} %compare_select_fusion.2, f32[4,128,2048]{2,1,0:T(8,128)} %pad_maximum_fusion.3), kind=kCustom, calls=%fused_computation.1.clone.1 | custom fusion | flops 1048576 | bytes 12582928 | tf_op jit(solution)/shard_map/while/body/eval_jaxpr/scatter-add | solution.py:98
  277.4 5.0 convert.4
  284.0 8.5 %collective-permute-start.4 = (bf16[128,2048]{1,0:T(8,128)(2,1)S(1)}, bf16[128,2048]{1,0:T(8,128)(2,1)S(1)}, u32[]{:S(2)}, u32[]{:S(2)}) collective-permute-start(bf16[128,2048]{1,0:T(8,128)(2,1)S(1)} %get-tuple-element.135), channel_id=1, source_target_pairs={{0,1},{1,2},{2,3},{3,4},{4,5},{5,6},{6,7},{7,8},{8,9},{9,10},{10,1... | collective-permute-start | bytes 1572872 | tf_op jit(solution)/shard_map/ppermute | solution.py:33
  292.5 4.8 convolution_bitcast_fusion.4
  297.3 3.8 slice.76
  302.3 2.3 fusion.28
  304.7 4.0 convert_element_type.55
  310.7 6.8 %convolution_bitcast_fusion.3 = f32[1024,2048]{0,1:T(8,128)} fusion(bf16[1024,2048]{1,0:T(8,128)(2,1)S(1)} %convert_element_type.55, bf16[1,1024,1024]{2,1,0:T(8,128)(2,1)S(1)} %copy-done), kind=kOutput, calls=%fused_computation.30 | convolution fusion | flops 4294967296 | bytes 14680064 | tf_op jit(solution)/shard_map/dot_general | solution.py:118
  317.5 12.1 %maximum_multiply_fusion = f32[1024,3072]{0,1:T(8,128)} fusion(f32[1024,2048]{0,1:T(8,128)} %convolution_bitcast_fusion.3, f32[1024,1024]{0,1:T(8,128)} %convolution_bitcast_fusion.4), kind=kLoop, calls=%fused_computation.28 | loop fusion | flops 6291456 | bytes 25165824 | tf_op jit(solution)/shard_map/div | solution.py:121
  329.6 12.6 %copy.37 = f32[1024,3072]{1,0:T(8,128)} copy(f32[1024,3072]{0,1:T(8,128)} %maximum_multiply_fusion) | data formatting | bytes 25165824
  343.4 4.0 fusion.27
  347.4 2.4 fusion.19
  349.8 3.7 fusion.18
  353.5 214.2 %reduce-scatter.4.cloned.1.call-done = f32[8,3072]{1,0:T(8,128)} async-done(((f32[1024,3072]{1,0:T(8,128)}), f32[8,3072]{1,0:T(8,128)}) %reduce-scatter.4.cloned.1.call-update) | async-done | bytes 98320
  (141 shorter events, 67.9 us)
Async XLA Ops:
  7.2 6.6 %copy-start = (bf16[1,1024,1024]{2,1,0:T(8,128)(2,1)S(1)}, bf16[1,1024,1024]{2,1,0:T(8,128)(2,1)}, u32[]{:S(2)}) copy-start(bf16[1,1024,1024]{2,1,0:T(8,128)(2,1)} %param.14) | copy-start | bytes 6291460
  7.2 560.5 %reduce-scatter.4.cloned.1.call-start = ((), (), s32[]{:S(2)}) async-start(), calls=%async_computation.1 | async-start | bytes 12681216
  9.6 17.9 %copy-start.12 = (s32[16]{0:T(128)S(1)}, s32[16]{0:T(128)}, u32[]{:S(2)}) copy-start(s32[16]{0:T(128)} %param.20) | copy-start | bytes 196
  9.6 26.9 %collective-permute-start.2 = (bf16[1,512,1024]{1,2,0:T(8,128)(2,1)}, bf16[1,512,1024]{1,2,0:T(8,128)(2,1)S(1)}, u32[]{:S(2)}, u32[]{:S(2)}) collective-permute-start(bf16[1,512,1024]{1,2,0:T(8,128)(2,1)} %copy.32), channel_id=1, source_target_pairs={{0,96},{32,0},{64,32},{96,64},{1,97},{33,1},{65,33},{97,65},{2,98}... | collective-permute-start | bytes 3145736 | tf_op jit(solution)/shard_map/ppermute | solution.py:14
  20.7 2.0 copy-start.3
  23.8 8.1 %collective-permute-start = (bf16[128,2048]{1,0:T(8,128)(2,1)}, bf16[128,2048]{1,0:T(8,128)(2,1)}, u32[]{:S(2)}, u32[]{:S(2)}) collective-permute-start(bf16[128,2048]{1,0:T(8,128)(2,1)} %get-tuple-element.137), channel_id=1, source_target_pairs={{0,1},{1,2},{2,3},{3,4},{4,5},{5,6},{6,7},{7,8},{8,9},{9,10},{10,1... | collective-permute-start | bytes 1572872 | tf_op jit(solution)/shard_map/ppermute | solution.py:24
  26.1 5.8 %collective-permute-start.1 = (bf16[128,2048]{1,0:T(8,128)(2,1)}, bf16[128,2048]{1,0:T(8,128)(2,1)}, u32[]{:S(2)}, u32[]{:S(2)}) collective-permute-start(bf16[128,2048]{1,0:T(8,128)(2,1)} %get-tuple-element.138), channel_id=1, source_target_pairs={{1,0},{2,1},{3,2},{4,3},{5,4},{6,5},{7,6},{8,7},{9,8},{10,9},{11,1... | collective-permute-start | bytes 1572872 | tf_op jit(solution)/shard_map/ppermute | solution.py:25
  27.6 4.3 copy-start.4
  41.8 3.2 copy-start.7
  62.9 2.7 copy-start.1
  74.0 4.5 copy-start.2
  91.6 9.0 %copy-start.8 = (bf16[512,1024]{0,1:T(8,128)(2,1)S(1)}, bf16[512,1024]{0,1:T(8,128)(2,1)}, u32[]{:S(2)}) copy-start(bf16[512,1024]{0,1:T(8,128)(2,1)} %copy-done.7) | copy-start | bytes 3145732 | tf_op jit(solution)/shard_map/while
  100.7 3.2 copy-start.7
  121.8 2.7 copy-start.1
  132.9 4.5 copy-start.2
  150.5 9.1 %copy-start.8 = (bf16[512,1024]{0,1:T(8,128)(2,1)S(1)}, bf16[512,1024]{0,1:T(8,128)(2,1)}, u32[]{:S(2)}) copy-start(bf16[512,1024]{0,1:T(8,128)(2,1)} %copy-done.7) | copy-start | bytes 3145732 | tf_op jit(solution)/shard_map/while
  159.6 3.2 copy-start.7
  180.7 2.7 copy-start.1
  191.8 4.5 copy-start.2
  209.4 9.1 %copy-start.8 = (bf16[512,1024]{0,1:T(8,128)(2,1)S(1)}, bf16[512,1024]{0,1:T(8,128)(2,1)}, u32[]{:S(2)}) copy-start(bf16[512,1024]{0,1:T(8,128)(2,1)} %copy-done.7) | copy-start | bytes 3145732 | tf_op jit(solution)/shard_map/while
  218.5 3.2 copy-start.7
  239.6 2.7 copy-start.1
  250.7 4.5 copy-start.2
  268.3 9.1 %copy-start.8 = (bf16[512,1024]{0,1:T(8,128)(2,1)S(1)}, bf16[512,1024]{0,1:T(8,128)(2,1)}, u32[]{:S(2)}) copy-start(bf16[512,1024]{0,1:T(8,128)(2,1)} %copy-done.7) | copy-start | bytes 3145732 | tf_op jit(solution)/shard_map/while
  277.4 20.0 %slice-start = ((s8[10485760]{0:T(1024)(128)(4,1)}), s8[4194304]{0:T(1024)(128)(4,1)S(1)}, s32[]{:S(2)}) async-start(s8[10485760]{0:T(1024)(128)(4,1)} %bitcast.136), calls=%async_computation.2 | async-start | bytes 8388608
  277.4 20.0 %slice-start.1 = ((s8[10485760]{0:T(1024)(128)(4,1)}), s8[2097152]{0:T(1024)(128)(4,1)S(1)}, s32[]{:S(2)}) async-start(s8[10485760]{0:T(1024)(128)(4,1)} %bitcast.136), calls=%async_computation.3 | async-start | bytes 4194304
  282.3 15.0 %slice-start.2 = ((s8[10485760]{0:T(1024)(128)(4,1)}), s8[4194304]{0:T(1024)(128)(4,1)S(1)}, s32[]{:S(2)}) async-start(s8[10485760]{0:T(1024)(128)(4,1)} %bitcast.136), calls=%async_computation.4 | async-start | bytes 8388608
  282.5 18.7 %collective-permute-start.3 = (bf16[128,2048]{1,0:T(8,128)(2,1)S(1)}, bf16[128,2048]{1,0:T(8,128)(2,1)S(1)}, u32[]{:S(2)}, u32[]{:S(2)}) collective-permute-start(bf16[128,2048]{1,0:T(8,128)(2,1)S(1)} %get-tuple-element.136), channel_id=1, source_target_pairs={{1,0},{2,1},{3,2},{4,3},{5,4},{6,5},{7,6},{8,7},{9,8},{10,9},{11,1... | collective-permute-start | bytes 1572872 | tf_op jit(solution)/shard_map/ppermute | solution.py:33
  284.0 18.3 %collective-permute-start.4 = (bf16[128,2048]{1,0:T(8,128)(2,1)S(1)}, bf16[128,2048]{1,0:T(8,128)(2,1)S(1)}, u32[]{:S(2)}, u32[]{:S(2)}) collective-permute-start(bf16[128,2048]{1,0:T(8,128)(2,1)S(1)} %get-tuple-element.135), channel_id=1, source_target_pairs={{0,1},{1,2},{2,3},{3,4},{4,5},{5,6},{6,7},{7,8},{8,9},{9,10},{10,1... | collective-permute-start | bytes 1572872 | tf_op jit(solution)/shard_map/ppermute | solution.py:33
  308.7 2.0 copy-start.5
  342.2 1.2 copy-start.9
  343.4 4.0 copy-start.6
  343.4 4.0 copy-start.10
  347.4 2.4 copy-start.11
Sparse Core Ops, SparseCore 0:
  342.4 225.2 reduce-scatter.3
where the time goes:
time: 576 us; the launch traced here: 575 us
  waiting for transfers between devices  215 us (37%)
  local copies, waits for them, and re-layouts  137 us (24%)
  other arithmetic  98.5 us (17%)
  matrix products  87 us (15%)
  starting transfers between devices  17.9 us (3%)
  between operations  14.2 us (2%)
    unnamed x2, waiting for transfers between devices  214 us
    concatenate x16, local copies, waits for them, and re-layouts, attend(): return (dquery, jnp.concatenate([dkey, dvalue], axis=1))  46.6 us
    scatter-add x4, other arithmetic, step(): acc = acc.at[ids].add(dkv.reshape(K, BLOCK, 2 * width))  36.2 us
    unnamed x26, local copies, waits for them, and re-layouts  20.2 us
    sub x4, matrix products, attend(): expo = jnp.where(live[None], jnp.exp(shifted - top), 0.0)  18.8 us
    concatenate x4, other arithmetic, attend(): return (dquery, jnp.concatenate([dkey, dvalue], axis=1))  18.7 us
    gather x4, local copies, waits for them, and re-layouts, step(): kv_rows = kv_blocks[ids].reshape(K * BLOCK, 2 * width)  17.9 us
    while x48, local copies, waits for them, and re-layouts  15.8 us
  transfers between devices with their start and end apart: 6, of which 2 were waited for; matrix products, arithmetic and copies ran while one was open for 6% of the time, Pallas kernels for 0%

commit v1 on v0

v1 whole, which is shorter than its diff:
```python
import jax
import jax.numpy as jnp
from jax import lax
from jax.experimental import pallas as pl
from jax.experimental.pallas import tpu as pltpu
from jax.sharding import PartitionSpec as P

LOG2E = 1.4426950408889634
F32, BF16 = jnp.float32, jnp.bfloat16

def nt(a, b):
    return lax.dot_general(a, b, (((1,), (1,)), ((), ())), preferred_element_type=F32)
def tn(a, b):
    return lax.dot_general(a, b, (((0,), (0,)), ((), ())), preferred_element_type=F32)
def nn(a, b):
    return lax.dot_general(a, b, (((1,), (0,)), ((), ())), preferred_element_type=F32)

def paired(x):
    left = lax.broadcasted_iota(jnp.int32, x.shape, 1) < 64
    zero = jnp.zeros_like(x)
    return jnp.concatenate([jnp.where(left, x, zero), jnp.where(left, zero, x)], axis=0)

def attend(ids_ref, m, cols, q_ref, a_ref, k_ref, v_ref, bias_ref, dq_ref, dk_part, dv_part):
    rows = pl.ds(m * 128, 128)
    starts = [pl.multiple_of(ids_ref[m * 4 + s] * 128, 128) for s in range(4)]
    keys = jnp.concatenate([k_ref[pl.ds(b, 128), cols] for b in starts], axis=0)
    values = jnp.concatenate([v_ref[pl.ds(b, 128), cols] for b in starts], axis=0)
    qq = paired(q_ref[rows, cols] * 0.125)
    aa = paired(a_ref[rows, cols])
    bias = bias_ref[m]
    bias = jnp.concatenate([bias, bias], axis=1)
    scores = nt(keys, qq) + bias
    top = jnp.max(scores, axis=0, keepdims=True)
    expo = jnp.exp2((scores - top) * LOG2E)
    probs = expo * (1.0 / jnp.sum(expo, axis=0, keepdims=True))
    probs_b = probs.astype(BF16)
    dprobs = nt(values, aa)
    delta = jnp.sum(probs_b.astype(F32) * dprobs, axis=0, keepdims=True)
    ds = (probs * (dprobs - delta)).astype(BF16)
    dv = nn(probs_b, aa)
    dk = nn(ds, qq)
    for s in range(4):
        dv_part[m * 4 + s] = dv[s * 128:(s + 1) * 128]
        dk_part[m * 4 + s] = dk[s * 128:(s + 1) * 128]
    dq = tn(keys, ds)
    dq = jnp.concatenate([dq[:64, :128], dq[64:, 128:]], axis=0) * 0.125
    dq_ref[rows, cols] = dq.T.astype(BF16)

def kernel(ids_ref, q_ref, a_ref, k_ref, v_ref, mask_ref, dq_ref, dk_ref, dv_ref, bias_ref, dk_part, dv_part):
    for e in range(16):
        bias_ref[e // 4, (e % 4) * 128:(e % 4 + 1) * 128, :] = (mask_ref[e].astype(F32).T - 1.0) * 1e30
    dk_part[16] = jnp.zeros((128, 128), F32)
    dv_part[16] = jnp.zeros((128, 128), F32)

    @pl.loop(0, 8)
    def _(pair):
        cols = pl.ds(pl.multiple_of(pair * 128, 128), 128)
        for m in range(4):
            attend(ids_ref, m, cols, q_ref, a_ref, k_ref, v_ref, bias_ref, dq_ref, dk_part, dv_part)

        @pl.loop(0, 10)
        def _(block):
            at = []
            for m in range(4):
                where = 16
                for s in range(4):
                    where = jnp.where(ids_ref[m * 4 + s] == block, m * 4 + s, where)
                at.append(where)
            rows = pl.ds(pl.multiple_of(block * 128, 128), 128)
            dk_ref[rows, cols] = ((dk_part[at[0]] + dk_part[at[1]]) + (dk_part[at[2]] + dk_part[at[3]])).astype(dk_ref.dtype)
            dv_ref[rows, cols] = ((dv_part[at[0]] + dv_part[at[1]]) + (dv_part[at[2]] + dv_part[at[3]])).astype(dv_ref.dtype)

def call(ids, q, a, k, v, mask):
    vm = pl.BlockSpec(memory_space=pltpu.VMEM)
    return pl.pallas_call(
        kernel,
        in_specs=[pl.BlockSpec(memory_space=pltpu.SMEM)] + [vm] * 5,
        out_specs=[vm] * 3,
        out_shape=[jax.ShapeDtypeStruct((512, 1024), BF16), jax.ShapeDtypeStruct((1280, 1024), F32), jax.ShapeDtypeStruct((1280, 1024), F32)],
        scratch_shapes=[pltpu.VMEM((4, 512, 128), F32), pltpu.VMEM((17, 128, 128), F32), pltpu.VMEM((17, 128, 128), F32)],
        compiler_params=pltpu.CompilerParams(vmem_limit_bytes=60 << 20),
    )(ids, q, a, k, v, mask)

def passed_along(value, axis, steps):
    count = lax.axis_size(axis)
    pairs = [(source, (source + steps) % count) for source in range(count)]
    return lax.ppermute(value, axis, pairs)


def with_halo(shard, sides, width):
    for axis, dim in sides:
        devices, length = (lax.axis_size(axis), shard.shape[dim])
        up = [(i, (i + 1) % devices) for i in range(devices - 1)]
        down = [(j, i) for i, j in up]
        last = lax.slice_in_dim(shard, length - width, length, axis=dim)
        initial = lax.slice_in_dim(shard, 0, width, axis=dim)
        before = lax.ppermute(last, axis, up)
        after = lax.ppermute(initial, axis, down)
        shard = jnp.concatenate([before, shard, after], axis=dim)
    return shard


def passed_along_2(shard, axis, by):
    devices = lax.axis_size(axis)
    pairs = [(i, i + by) for i in range(devices) if 0 <= i + by < devices]
    return lax.ppermute(shard, axis, pairs)


def times_transposed(left, weight):
    return lax.dot_general(
        left, weight, (((1,), (1,)), ((), ())), preferred_element_type=jnp.float32
    )


def on_device(grid_feat, mesh_feat, mesh_adjoint, w_query, w_key, w_value, block_grid, block_mask):
    arrived = passed_along(mesh_adjoint, "sec", -1)[0]
    feats = grid_feat[0]
    nodes = mesh_feat[0]
    band = lax.axis_index("space")
    own_k = nn(feats, w_key).astype(BF16)
    own_v = nn(feats, w_value).astype(BF16)
    keys = with_halo(own_k, (("space", 0),), 128)
    values = with_halo(own_v, (("space", 0),), 128)
    queries = nn(nodes, w_query).astype(BF16)
    local_ids = block_grid - band * 8 + 1
    dquery, dkey, dvalue = call(local_ids, queries, arrived, keys, values, block_mask)

    def folded(acc):
        above = passed_along_2(acc[:128].astype(BF16), "space", -1).astype(F32)
        below = passed_along_2(acc[-128:].astype(BF16), "space", 1).astype(F32)
        core = acc[128:-128]
        core = core.at[-128:].add(above)
        core = core.at[:128].add(below)
        return core.astype(BF16)

    dkey = folded(dkey)
    dvalue = folded(dvalue)
    grid_grad = (times_transposed(dkey, w_key) + times_transposed(dvalue, w_value)).astype(BF16)
    mesh_grad = times_transposed(dquery, w_query).astype(BF16)
    terms = jnp.concatenate([tn(nodes, dquery), tn(feats, dkey), tn(feats, dvalue)], axis=1) * 0.25
    w_grad = lax.psum_scatter(terms.astype(BF16), ("sec", "space"), scatter_dimension=0, tiled=True)
    return (grid_grad[None], mesh_grad[None], w_grad.astype(F32))


def solution(mesh):
    placed = (
        P("sec", "space", None),
        P("sec", "space", None),
        P("sec", "space", None),
        P(),
        P(),
        P(),
        P("space"),
        P("space", None, None),
    )
    return jax.shard_map(
        on_device,
        mesh=mesh,
        in_specs=placed,
        out_specs=(P("sec", "space", None), P("sec", "space", None), P(("sec", "space"), None)),
        check_vma=False,
    )
```

time: 576 us -> 341 us (0.59)
  local copies, waits for them, and re-layouts: 137 us -> 17.8 us
  other arithmetic: 98.5 us -> 14.9 us
  matrix products: 87 us -> 23.1 us
  Pallas kernels: 0 us -> 33.7 us
  starting transfers between devices: 17.9 us -> 25.6 us
    concatenate x16 -> x0, local copies, waits for them, and re-layouts: 46.6 us -> none  [attend(): return (dquery, jnp.concatenate([dkey, dvalue], axis=1))]
    dot_general x24 -> x6, matrix products: 58.1 us -> 14.8 us  [the longest x3 8.5 us: nn(): lax.dot_general(a, b, (((1,), (0,)), ((), ())), preferred_element_type=F32)]
    scatter-add x6 -> x4, other arithmetic: 39.7 us -> 0.37 us  [the longest x2 0.24 us: folded(): core = core.at[:128].add(below)]
    pallas_call x0 -> x1, Pallas kernels: none -> 33.7 us  [call(): pl.pallas_call(kernel, in_specs=[pl.BlockSpec(memory_space=pltpu.SMEM)] +...]
    sub x4 -> x0, matrix products: 18.8 us -> none  [attend(): expo = jnp.where(live[None], jnp.exp(shifted - top), 0.0)]
    concatenate x4 -> x0, other arithmetic: 18.7 us -> none  [attend(): return (dquery, jnp.concatenate([dkey, dvalue], axis=1))]
    gather x4 -> x0, local copies, waits for them, and re-layouts: 17.9 us -> none  [step(): kv_rows = kv_blocks[ids].reshape(K * BLOCK, 2 * width)]
    while x48 -> x0, local copies, waits for them, and re-layouts: 15.8 us -> none
  transfers between devices with their start and end apart: 6 -> 10, of which waited for: 2 -> 1; matrix products, arithmetic and copies ran while one was open for 6% -> 9% of each run, Pallas kernels for 0% -> 0%
where the time goes in v1:
time: 341 us; the launch traced here: 340 us
  waiting for transfers between devices  211 us (62%)
  Pallas kernels  33.7 us (10%)
  starting transfers between devices  25.6 us (8%)
  matrix products  23.1 us (7%)
  local copies, waits for them, and re-layouts  17.8 us (5%)
  other arithmetic  14.9 us (4%)
  between operations  14.4 us (4%)
    unnamed x2, waiting for transfers between devices  211 us
    pallas_call x1, Pallas kernels, call(): pl.pallas_call(kernel, in_specs=[pl.BlockSpec(memory_space=pltpu.SMEM)] +...  33.7 us
    unnamed x47, local copies, waits for them, and re-layouts  14.8 us
    ppermute x4, starting transfers between devices, passed_along_2(): return lax.ppermute(shard, axis, pairs)  11 us
    dot_general x3, matrix products, nn(): lax.dot_general(a, b, (((1,), (0,)), ((), ())), preferred_element_type=F32)  8.5 us
    dot_general x3, matrix products, times_transposed(): lax.dot_general(left, weight, (((1,), (1,)), ((), ())), preferred_element...  8.34 us
    ppermute x2, starting transfers between devices, with_halo(): before = lax.ppermute(last, axis, up)  7.78 us
  transfers between devices with their start and end apart: 10, of which 1 were waited for; matrix products, arithmetic and copies ran while one was open for 9% of the time, Pallas kernels for 0%

profile of v1, /device:TPU:0, one launch (start us, length us, event | category | flops | bytes accessed | tf_op | source)
XLA Modules:
  0.0 340.1 jit_solution(6470345066138233664)
XLA Ops:
  7.2 0.0 copy-start
  7.2 0.0 reduce-scatter.4.cloned.1.call-start
  7.2 0.0 copy-start.16
  7.2 4.2 %collective-permute-start = (bf16[1,512,1024]{2,1,0:T(8,128)(2,1)}, bf16[1,512,1024]{2,1,0:T(8,128)(2,1)S(1)}, u32[]{:S(2)}, u32[]{:S(2)}) collective-permute-start(bf16[1,512,1024]{2,1,0:T(8,128)(2,1)} %param.18), channel_id=1, source_target_pairs={{0,96},{32,0},{64,32},{96,64},{1,97},{33,1},{65,33},{97,65},{2,98}... | collective-permute-start | bytes 3145736 | tf_op jit(solution)/shard_map/ppermute | solution.py:87
  11.4 0.0 copy-done
  11.4 3.9 %fusion.8 = bf16[1024,1024]{1,0:T(8,128)(2,1)S(1)} fusion(bf16[1024,1024]{1,0:T(8,128)(2,1)} %param.20, bf16[1,1024,1024]{2,1,0:T(8,128)(2,1)S(1)} %copy-done), kind=kOutput, calls=%fused_computation.15 | convolution fusion | flops 2148532224 | bytes 6291456 | tf_op jit(solution)/shard_map/dot_general | solution.py:16
  15.4 0.0 copy-start.7
  15.4 0.9 fusion.27
  16.3 1.3 collective-permute-start.2
  17.5 0.0 copy-start.12
  17.6 0.0 copy-start.14
  17.6 4.0 %collective-permute-start.1 = (bf16[128,1024]{1,0:T(8,128)(2,1)}, bf16[128,1024]{1,0:T(8,128)(2,1)}, u32[]{:S(2)}, u32[]{:S(2)}) collective-permute-start(bf16[128,1024]{1,0:T(8,128)(2,1)} %get-tuple-element.69), channel_id=1, source_target_pairs={{0,1},{1,2},{2,3},{3,4},{4,5},{5,6},{6,7},{7,8},{8,9},{9,10},{10,1... | collective-permute-start | bytes 786440 | tf_op jit(solution)/shard_map/ppermute | solution.py:97
  21.6 2.4 fusion.11
  23.9 0.0 copy-done.7
  23.9 0.0 copy-start.8
  24.0 0.9 fusion.26
  24.8 1.3 collective-permute-start.4
  26.1 0.0 copy-start.19
  26.1 3.8 %collective-permute-start.3 = (bf16[128,1024]{1,0:T(8,128)(2,1)}, bf16[128,1024]{1,0:T(8,128)(2,1)}, u32[]{:S(2)}, u32[]{:S(2)}) collective-permute-start(bf16[128,1024]{1,0:T(8,128)(2,1)} %get-tuple-element.67), channel_id=1, source_target_pairs={{0,1},{1,2},{2,3},{3,4},{4,5},{5,6},{6,7},{7,8},{8,9},{9,10},{10,1... | collective-permute-start | bytes 786440 | tf_op jit(solution)/shard_map/ppermute | solution.py:97
  29.9 2.2 convolution_convert_fusion.1.q_ref
  32.2 0.5 subtract_add_fusion.ids_ref
  32.7 0.0 collective-permute-done.2
  32.7 0.0 collective-permute-done.1
  32.7 3.6 %pad_maximum_fusion.k_ref = bf16[1280,1024]{1,0:T(8,128)(2,1)} fusion(bf16[128,1024]{1,0:T(8,128)(2,1)S(1)} %collective-permute-done.2, bf16[1024,1024]{1,0:T(8,128)(2,1)} %copy-done.7, bf16[128,1024]{1,0:T(8,128)(2,1)} %collective-permute-done.1), kind=kLoop, calls=%fused_computation.3 | loop fusion | flops 7864320 | bytes 5242880 | tf_op jit(solution)/shard_map/concatenate | solution.py:99
  36.2 0.0 collective-permute-done.4
  36.2 0.0 collective-permute-done.3
  36.3 2.8 pad_maximum_fusion.1.v_ref
  39.0 0.0 collective-permute-done
  39.0 1.0 copy-done.11
  40.0 33.7 %shard_map.103 = (bf16[512,1024]{1,0:T(8,128)(2,1)}, f32[1280,1024]{1,0:T(8,128)}, f32[1280,1024]{1,0:T(8,128)}) custom-call(s32[16]{0:T(128)} %subtract_add_fusion.ids_ref, bf16[512,1024]{1,0:T(8,128)(2,1)} %convolution_convert_fusion.1.q_ref, bf16[512,1024]{1,0:T(8,128)(2,1)} %bitcast.40, bf16[1280,1024]{1,0:T(8,128)(2,1)} %pad_maximum_fusion.k_ref, ...), custom_call_target="tpu_custom_call" | custom-call | tf_op jit(solution)/shard_map/pallas_call | solution.py:75
  73.7 3.0 convert.9
  76.8 1.3 collective-permute-start.7
  78.1 3.6 %collective-permute-start.8 = (bf16[128,1024]{1,0:T(8,128)(2,1)S(1)}, bf16[128,1024]{1,0:T(8,128)(2,1)S(1)}, u32[]{:S(2)}, u32[]{:S(2)}) collective-permute-start(bf16[128,1024]{1,0:T(8,128)(2,1)S(1)} %get-tuple-element.65), channel_id=1, source_target_pairs={{0,1},{1,2},{2,3},{3,4},{4,5},{5,6},{6,7},{7,8},{8,9},{9,10},{10,1... | collective-permute-start | bytes 786440 | tf_op jit(solution)/shard_map/ppermute | solution.py:106
  81.7 0.0 copy-start.13
  81.7 0.0 slice-start
  81.7 0.4 convert.8
  82.1 0.0 slice-start.1
  82.2 1.6 collective-permute-start.5
  83.7 4.6 %collective-permute-start.6 = (bf16[128,1024]{1,0:T(8,128)(2,1)S(1)}, bf16[128,1024]{1,0:T(8,128)(2,1)S(1)}, u32[]{:S(2)}, u32[]{:S(2)}) collective-permute-start(bf16[128,1024]{1,0:T(8,128)(2,1)S(1)} %get-tuple-element.63), channel_id=1, source_target_pairs={{0,1},{1,2},{2,3},{3,4},{4,5},{5,6},{6,7},{7,8},{8,9},{9,10},{10,1... | collective-permute-start | bytes 786440 | tf_op jit(solution)/shard_map/ppermute | solution.py:106
  88.3 1.3 convolution_bitcast_fusion.2
  89.7 0.6 slice.121
  90.3 0.6 slice.116
  90.8 0.0 collective-permute-done.7
  90.9 0.1 add_dynamic-update-slice_fusion
  90.9 0.0 collective-permute-done.8
  90.9 0.1 fusion.22
  91.1 2.5 convolution_bitcast_fusion
  93.6 0.0 collective-permute-done.5
  93.6 0.1 add_dynamic-update-slice_fusion.1
  93.7 0.0 collective-permute-done.6
  93.7 0.1 fusion.23
  93.8 2.5 convolution_bitcast_fusion.1
  96.3 4.2 %fusion = bf16[1024,3072]{0,1:T(8,128)(2,1)} fusion(f32[1024,1024]{0,1:T(8,128)S(1)} %convolution_bitcast_fusion, f32[1024,1024]{0,1:T(8,128)S(1)} %convolution_bitcast_fusion.1, f32[1024,1024]{0,1:T(8,128)S(1)} %convolution_bitcast_fusion.2), kind=kLoop, calls=%fused_computation.1 | loop fusion | flops 12582912 | bytes 18874368 | tf_op jit(solution)/shard_map/convert_element_type | solution.py:141
  100.5 8.6 %copy.13 = bf16[1024,3072]{1,0:T(8,128)(2,1)} copy(bf16[1024,3072]{0,1:T(8,128)(2,1)} %fusion) | data formatting | bytes 12582912
  109.2 0.0 reduce-scatter.4.cloned.1.call-update
  109.2 1.6 copy-done.15
  110.8 2.3 fusion.14
  113.0 1.0 copy-done.17
  114.0 2.4 fusion.18
  116.4 0.5 copy-done.18
  116.9 3.7 %fusion.1 = bf16[1,1024,1024]{2,1,0:T(8,128)(2,1)} fusion(f32[1024,1024]{1,0:T(8,128)S(1)} %fusion.18, bf16[1024,1024]{1,0:T(8,128)(2,1)S(1)} %copy-done.18, f32[1024,1024]{1,0:T(8,128)S(1)} %copy-done.4), kind=kOutput, calls=%fused_computation.8 | convolution fusion | flops 2150629376 | bytes 12582912 | tf_op jit(solution)/shard_map/dot_general | solution.py:110
  120.6 210.6 %reduce-scatter.4.cloned.1.call-done = bf16[8,3072]{1,0:T(8,128)(2,1)} async-done(((bf16[1024,3072]{1,0:T(8,128)(2,1)}), bf16[8,3072]{1,0:T(8,128)(2,1)}) %reduce-scatter.4.cloned.1.call-update) | async-done | bytes 49168
  331.2 1.2 copy.14
  332.3 0.9 copy.12
  (31 shorter events, 0.1 us)
Async XLA Ops:
  7.2 4.3 %copy-start = (bf16[1,1024,1024]{2,1,0:T(8,128)(2,1)S(1)}, bf16[1,1024,1024]{2,1,0:T(8,128)(2,1)}, u32[]{:S(2)}) copy-start(bf16[1,1024,1024]{2,1,0:T(8,128)(2,1)} %param.16) | copy-start | bytes 6291460
  7.2 324.0 %reduce-scatter.4.cloned.1.call-start = ((), (), s32[]{:S(2)}) async-start(), calls=%async_computation.1 | async-start | bytes 6340608
  7.2 14.3 %copy-start.16 = (bf16[1024,1024]{1,0:T(8,128)(2,1)S(1)}, bf16[1024,1024]{1,0:T(8,128)(2,1)}, u32[]{:S(2)}) copy-start(bf16[1024,1024]{1,0:T(8,128)(2,1)} %param.21) | copy-start | bytes 6291460
  7.2 31.8 %collective-permute-start = (bf16[1,512,1024]{2,1,0:T(8,128)(2,1)}, bf16[1,512,1024]{2,1,0:T(8,128)(2,1)S(1)}, u32[]{:S(2)}, u32[]{:S(2)}) collective-permute-start(bf16[1,512,1024]{2,1,0:T(8,128)(2,1)} %param.18), channel_id=1, source_target_pairs={{0,96},{32,0},{64,32},{96,64},{1,97},{33,1},{65,33},{97,65},{2,98}... | collective-permute-start | bytes 3145736 | tf_op jit(solution)/shard_map/ppermute | solution.py:87
  15.4 8.6 %copy-start.7 = (bf16[1024,1024]{1,0:T(8,128)(2,1)}, bf16[1024,1024]{1,0:T(8,128)(2,1)S(1)}, u32[]{:S(2)}) copy-start(bf16[1024,1024]{1,0:T(8,128)(2,1)S(1)} %fusion.8) | copy-start | bytes 6291460
  16.3 16.4 %collective-permute-start.2 = (bf16[128,1024]{1,0:T(8,128)(2,1)}, bf16[128,1024]{1,0:T(8,128)(2,1)S(1)}, u32[]{:S(2)}, u32[]{:S(2)}) collective-permute-start(bf16[128,1024]{1,0:T(8,128)(2,1)} %get-tuple-element.70), channel_id=1, source_target_pairs={{1,0},{2,1},{3,2},{4,3},{5,4},{6,5},{7,6},{8,7},{9,8},{10,9},{11,1... | collective-permute-start | bytes 786440 | tf_op jit(solution)/shard_map/ppermute | solution.py:98
  17.5 12.4 %copy-start.12 = (bf16[1,512,1024]{2,1,0:T(8,128)(2,1)S(1)}, bf16[1,512,1024]{2,1,0:T(8,128)(2,1)}, u32[]{:S(2)}) copy-start(bf16[1,512,1024]{2,1,0:T(8,128)(2,1)} %param.17) | copy-start | bytes 3145732
  17.6 12.4 %copy-start.14 = (bf16[1024,1024]{1,0:T(8,128)(2,1)S(1)}, bf16[1024,1024]{1,0:T(8,128)(2,1)}, u32[]{:S(2)}) copy-start(bf16[1024,1024]{1,0:T(8,128)(2,1)} %param.19) | copy-start | bytes 6291460
  17.6 15.1 %collective-permute-start.1 = (bf16[128,1024]{1,0:T(8,128)(2,1)}, bf16[128,1024]{1,0:T(8,128)(2,1)}, u32[]{:S(2)}, u32[]{:S(2)}) collective-permute-start(bf16[128,1024]{1,0:T(8,128)(2,1)} %get-tuple-element.69), channel_id=1, source_target_pairs={{0,1},{1,2},{2,3},{3,4},{4,5},{5,6},{6,7},{7,8},{8,9},{9,10},{10,1... | collective-permute-start | bytes 786440 | tf_op jit(solution)/shard_map/ppermute | solution.py:97
  23.9 8.2 %copy-start.8 = (bf16[1024,1024]{1,0:T(8,128)(2,1)}, bf16[1024,1024]{1,0:T(8,128)(2,1)S(1)}, u32[]{:S(2)}) copy-start(bf16[1024,1024]{1,0:T(8,128)(2,1)S(1)} %fusion.11) | copy-start | bytes 6291460
  24.8 11.4 %collective-permute-start.4 = (bf16[128,1024]{1,0:T(8,128)(2,1)}, bf16[128,1024]{1,0:T(8,128)(2,1)}, u32[]{:S(2)}, u32[]{:S(2)}) collective-permute-start(bf16[128,1024]{1,0:T(8,128)(2,1)} %get-tuple-element.68), channel_id=1, source_target_pairs={{1,0},{2,1},{3,2},{4,3},{5,4},{6,5},{7,6},{8,7},{9,8},{10,9},{11,1... | collective-permute-start | bytes 786440 | tf_op jit(solution)/shard_map/ppermute | solution.py:98
  26.1 6.0 %copy-start.19 = (s32[16]{0:T(128)S(1)}, s32[16]{0:T(128)}, u32[]{:S(2)}) copy-start(s32[16]{0:T(128)} %param.22) | copy-start | bytes 196
  26.1 10.1 %collective-permute-start.3 = (bf16[128,1024]{1,0:T(8,128)(2,1)}, bf16[128,1024]{1,0:T(8,128)(2,1)}, u32[]{:S(2)}, u32[]{:S(2)}) collective-permute-start(bf16[128,1024]{1,0:T(8,128)(2,1)} %get-tuple-element.67), channel_id=1, source_target_pairs={{0,1},{1,2},{2,3},{3,4},{4,5},{5,6},{6,7},{7,8},{8,9},{9,10},{10,1... | collective-permute-start | bytes 786440 | tf_op jit(solution)/shard_map/ppermute | solution.py:97
  32.7 3.6 %copy-start.9 = (bf16[1024,1024]{1,0:T(8,128)(2,1)S(1)}, bf16[1024,1024]{1,0:T(8,128)(2,1)}, u32[]{:S(2)}) copy-start(bf16[1024,1024]{1,0:T(8,128)(2,1)} %copy-done.8) | copy-start | bytes 6291460
  39.0 1.0 copy-start.11
  73.7 8.0 %copy-start.2 = (f32[1280,1024]{1,0:T(8,128)S(1)}, f32[1280,1024]{1,0:T(8,128)}, u32[]{:S(2)}) copy-start(f32[1280,1024]{1,0:T(8,128)} %get-tuple-element.54) | copy-start | bytes 15728644
  76.8 14.1 %collective-permute-start.7 = (bf16[128,1024]{1,0:T(8,128)(2,1)S(1)}, bf16[128,1024]{1,0:T(8,128)(2,1)S(1)}, u32[]{:S(2)}, u32[]{:S(2)}) collective-permute-start(bf16[128,1024]{1,0:T(8,128)(2,1)S(1)} %get-tuple-element.66), channel_id=1, source_target_pairs={{1,0},{2,1},{3,2},{4,3},{5,4},{6,5},{7,6},{8,7},{9,8},{10,9},{11,1... | collective-permute-start | bytes 786440 | tf_op jit(solution)/shard_map/ppermute | solution.py:106
  78.1 12.9 %collective-permute-start.8 = (bf16[128,1024]{1,0:T(8,128)(2,1)S(1)}, bf16[128,1024]{1,0:T(8,128)(2,1)S(1)}, u32[]{:S(2)}, u32[]{:S(2)}) collective-permute-start(bf16[128,1024]{1,0:T(8,128)(2,1)S(1)} %get-tuple-element.65), channel_id=1, source_target_pairs={{0,1},{1,2},{2,3},{3,4},{4,5},{5,6},{6,7},{7,8},{8,9},{9,10},{10,1... | collective-permute-start | bytes 786440 | tf_op jit(solution)/shard_map/ppermute | solution.py:106
  81.6 6.7 %copy-start.10 = (bf16[512,1024]{1,0:T(8,128)(2,1)S(1)}, bf16[512,1024]{1,0:T(8,128)(2,1)}, u32[]{:S(2)}) copy-start(bf16[512,1024]{1,0:T(8,128)(2,1)} %get-tuple-element.56) | copy-start | bytes 3145732
  81.7 6.7 %copy-start.13 = (bf16[1,512,1024]{2,1,0:T(8,128)(2,1)S(1)}, bf16[1,512,1024]{2,1,0:T(8,128)(2,1)}, u32[]{:S(2)}) copy-start(bf16[1,512,1024]{2,1,0:T(8,128)(2,1)} %param.17) | copy-start | bytes 3145732
  81.7 8.0 %slice-start = ((s8[5242880]{0:T(1024)(128)(4,1)}), s8[4194304]{0:T(1024)(128)(4,1)S(1)}, s32[]{:S(2)}) async-start(s8[5242880]{0:T(1024)(128)(4,1)} %bitcast.38), calls=%async_computation.2 | async-start | bytes 8388608
  82.1 7.6 %slice-start.1 = ((s8[5242880]{0:T(1024)(128)(4,1)}), s8[1048576]{0:T(1024)(128)(4,1)S(1)}, s32[]{:S(2)}) async-start(s8[5242880]{0:T(1024)(128)(4,1)} %bitcast.38), calls=%async_computation.3 | async-start | bytes 2097152
  82.2 11.4 %collective-permute-start.5 = (bf16[128,1024]{1,0:T(8,128)(2,1)S(1)}, bf16[128,1024]{1,0:T(8,128)(2,1)S(1)}, u32[]{:S(2)}, u32[]{:S(2)}) collective-permute-start(bf16[128,1024]{1,0:T(8,128)(2,1)S(1)} %get-tuple-element.64), channel_id=1, source_target_pairs={{1,0},{2,1},{3,2},{4,3},{5,4},{6,5},{7,6},{8,7},{9,8},{10,9},{11,1... | collective-permute-start | bytes 786440 | tf_op jit(solution)/shard_map/ppermute | solution.py:106
  83.7 9.9 %collective-permute-start.6 = (bf16[128,1024]{1,0:T(8,128)(2,1)S(1)}, bf16[128,1024]{1,0:T(8,128)(2,1)S(1)}, u32[]{:S(2)}, u32[]{:S(2)}) collective-permute-start(bf16[128,1024]{1,0:T(8,128)(2,1)S(1)} %get-tuple-element.63), channel_id=1, source_target_pairs={{0,1},{1,2},{2,3},{3,4},{4,5},{5,6},{6,7},{7,8},{8,9},{9,10},{10,1... | collective-permute-start | bytes 786440 | tf_op jit(solution)/shard_map/ppermute | solution.py:106
  91.1 2.5 copy-start.5
  93.8 2.5 copy-start.3
  109.2 1.6 copy-start.15
  110.8 2.3 copy-start.6
  110.8 3.2 copy-start.17
  114.0 2.4 copy-start.4
  114.0 2.9 copy-start.18
  116.9 216.4 %copy-start.1 = (bf16[1,1024,1024]{2,1,0:T(8,128)(2,1)S(1)}, bf16[1,1024,1024]{2,1,0:T(8,128)(2,1)}, u32[]{:S(2)}) copy-start(bf16[1,1024,1024]{2,1,0:T(8,128)(2,1)} %param.16) | copy-start | bytes 6291460
Sparse Core Ops, SparseCore 0:
  109.3 221.7 reduce-scatter.3

commit v2 on v1

v2 whole, which is shorter than its diff:
```python
import jax
import jax.numpy as jnp
from jax import lax
from jax.experimental import pallas as pl
from jax.experimental.pallas import tpu as pltpu
from jax.sharding import PartitionSpec as P

F32, BF16 = jnp.float32, jnp.bfloat16
MESH = pl.DeviceIdType.MESH
D = 1024
GROUPS = 4
W = D // GROUPS
PAIRS = W // 128
BANDS = 32
ORDERS = ((0, 1, 2), (1, 2, 0), (2, 0, 1))


def nt(a, b):
    return lax.dot_general(a, b, (((1,), (1,)), ((), ())), preferred_element_type=F32)


def tn(a, b):
    return lax.dot_general(a, b, (((0,), (0,)), ((), ())), preferred_element_type=F32)


def nn(a, b):
    return lax.dot_general(a, b, (((1,), (0,)), ((), ())), preferred_element_type=F32)


def paired(x):
    left = lax.broadcasted_iota(jnp.int32, x.shape, 1) < 64
    zero = jnp.zeros_like(x)
    return jnp.concatenate([jnp.where(left, x, zero), jnp.where(left, zero, x)], axis=0)


def kernel(
    ids_ref, x_hbm, h_hbm, a_hbm, wq_hbm, wk_hbm, wv_hbm, mask_hbm,
    gg_hbm, mg_hbm, wg_hbm,
    x_ref, h_ref, xt_ref, ht_ref, w_ref, mask_ref, bias_ref, adj_ref, q_ref, k_ref, v_ref,
    dq_ref, dk_ref, dv_ref, dk_part, dv_part, edge_ref,
    kv_out, kv_in, dkv_out, dkv_in,
    term_ref, core_in, a_out, a_in, b_out, b_in, c_out, c_in, wg_ref, gg_ref, mg_ref,
    local_ref, lists_ref, load_sem, w_sem, out_sem, adj_sem, kv_sem, dkv_sem, core_sem, a_sem, b_sem, c_sem,
):
    sec = lax.axis_index("sec")
    band = lax.axis_index("space")
    core = band % 2
    gx = band // 8
    gy = (band // 2) % 4
    place = (sec, gx, gy)

    def space_of(x, y, c):
        return (x * 4 + y) * 2 + c

    def peer(axis, steps):
        z, x, y = place
        if axis == 0:
            return ((z + steps) % 4, band)
        if axis == 1:
            return (z, space_of((x + steps) % 4, y, core))
        return (z, space_of(x, (y + steps) % 4, core))

    sibling = (sec, space_of(gx, gy, 1 - core))
    up = (sec, (band + 1) % BANDS)
    down = (sec, (band + BANDS - 1) % BANDS)
    across = (sec, (band + BANDS + 2 * core - 1) % BANDS)

    def cols_of(g):
        return pl.ds(pl.multiple_of(g * W, W), W)

    def load(src, dst, i):
        return pltpu.make_async_copy(src, dst, load_sem.at[i])

    def load_w(g, i):
        return pltpu.make_async_copy(
            (wq_hbm, wk_hbm, wv_hbm)[i].at[:, cols_of(g)], w_ref.at[i, :, cols_of(g)], w_sem.at[g, i]
        )

    def remote(src, dst, sem, at, to):
        return pltpu.make_async_remote_copy(
            src_ref=src, dst_ref=dst, send_sem=sem.at[(0, *at)], recv_sem=sem.at[(1, *at)],
            device_id=to, device_id_type=MESH,
        )

    barrier = pltpu.get_barrier_semaphore()
    peers = [sibling, across] + [peer(axis, steps) for axis in range(3) for steps in (1, 2, 3)]
    for to in peers:
        pl.semaphore_signal(barrier, inc=1, device_id=to, device_id_type=MESH)
    load(x_hbm, x_ref, 0).start()
    for i in (1, 2):
        load_w(0, i).start()
    load(h_hbm, h_ref, 1).start()
    load_w(0, 0).start()
    load(mask_hbm, mask_ref, 2).start()
    for g in range(1, GROUPS):
        for i in range(3):
            load_w(g, i).start()
    pl.semaphore_wait(barrier, len(peers))

    def adjoint(g):
        return remote(a_hbm.at[:, cols_of(g)], adj_ref.at[g], adj_sem, (g,), peer(0, 3))

    for g in range(GROUPS):
        adjoint(g).start()

    def halo(g, side):
        return remote(kv_out.at[g, side], kv_in.at[g, 1 - side], kv_sem, (g, side), (down, up)[side])

    def project(g):
        turn = g % 2
        for i in (1, 2):
            load_w(g, i).wait()
            own = nn(x_ref[...], w_ref[i, :, cols_of(g)]).astype(BF16)
            for b in range(8):
                (k_ref, v_ref)[i - 1][turn, b + 1] = own[b * 128:(b + 1) * 128]
            kv_out[g, 0, i - 1] = own[:128]
            kv_out[g, 1, i - 1] = own[896:]
        for side in range(2):
            halo(g, side).start()
        load_w(g, 0).wait()
        q_ref[turn] = (nn(h_ref[...], w_ref[0, :, cols_of(g)]).astype(BF16)) * 0.125

    load(x_hbm, x_ref, 0).wait()
    load(h_hbm, h_ref, 1).wait()
    project(0)

    @pl.loop(0, 8)
    def _(i):
        rows = pl.ds(pl.multiple_of(i * 128, 128), 128)
        xt_ref[:, rows] = x_ref[rows, :].T

    @pl.loop(0, 4)
    def _(i):
        rows = pl.ds(pl.multiple_of(i * 128, 128), 128)
        ht_ref[:, rows] = h_ref[rows, :].T

    load(mask_hbm, mask_ref, 2).wait()

    @pl.loop(0, 4)
    def _(m):
        for s in range(4):
            bias_ref[m, s * 128:(s + 1) * 128, :] = (mask_ref[m * 4 + s].astype(F32).T - 1.0) * 1e30

    dk_part[16] = jnp.zeros((128, 128), F32)
    dv_part[16] = jnp.zeros((128, 128), F32)

    for e in range(16):
        local_ref[e] = jnp.clip(ids_ref[e] - band * 8 + 1, 0, 9)
    for block in range(10):
        for m in range(4):
            at = 16
            for s in range(4):
                off = local_ref[m * 4 + s] - block
                at = at + (1 - jnp.minimum(off * off, 1)) * (m * 4 + s - 16)
            lists_ref[block * 4 + m] = jnp.clip(at, 0, 16)

    def attend(g, pair, m):
        turn = g % 2
        rows = slice(m * 128, (m + 1) * 128)
        cols = pl.ds(pl.multiple_of(pair * 128, 128), 128)
        blocks = [local_ref[m * 4 + s] for s in range(4)]
        keys = jnp.concatenate([k_ref[turn, b, :, cols] for b in blocks], axis=0)
        values = jnp.concatenate([v_ref[turn, b, :, cols] for b in blocks], axis=0)
        qq = paired(q_ref[turn, rows, cols])
        aa = paired(adj_ref[g, rows, cols])
        bias = bias_ref[m]
        bias = jnp.concatenate([bias, bias], axis=1)
        scores = nt(keys, qq) + bias
        top = jnp.max(scores, axis=0, keepdims=True)
        expo = jnp.exp(scores - top)
        probs = expo * (1.0 / jnp.sum(expo, axis=0, keepdims=True))
        probs_b = probs.astype(BF16)
        dprobs = nt(values, aa)
        delta = jnp.sum(probs_b.astype(F32) * dprobs, axis=0, keepdims=True)
        ds = (probs * (dprobs - delta)).astype(BF16)
        dv = nn(probs_b, aa)
        dk = nn(ds, qq)
        for s in range(4):
            dv_part[m * 4 + s] = dv[s * 128:(s + 1) * 128]
            dk_part[m * 4 + s] = dk[s * 128:(s + 1) * 128]
        dq = tn(keys, ds)
        dq = jnp.concatenate([dq[:64, :128], dq[64:, 128:]], axis=0) * 0.125
        dq_ref[g, rows, cols] = dq.T.astype(BF16)

    def gathered(part, block):
        found = [part[lists_ref[block * 4 + m]] for m in range(4)]
        return (found[0] + found[1]) + (found[2] + found[3])

    def attend_pair(g, pair):
        cols = pl.ds(pl.multiple_of(pair * 128, 128), 128)
        for m in range(4):
            attend(g, pair, m)
        for i, part in enumerate((dk_part, dv_part)):
            dkv_out[g, 0, i, :, cols] = gathered(part, 0).astype(BF16)
            dkv_out[g, 1, i, :, cols] = gathered(part, 9).astype(BF16)
            edge_ref[g % 2, 0, i, :, cols] = gathered(part, 1)
            edge_ref[g % 2, 1, i, :, cols] = gathered(part, 8)

        @pl.loop(1, 7)
        def _(block):
            rows = pl.ds(pl.multiple_of(block * 128, 128), 128)
            dk_ref[g, rows, cols] = gathered(dk_part, block + 1).astype(BF16)
            dv_ref[g, rows, cols] = gathered(dv_part, block + 1).astype(BF16)

    def back(g, side):
        return remote(dkv_out.at[g, side], dkv_in.at[g, 1 - side], dkv_sem, (g, side), (down, up)[side])

    def merge(g):
        for side in range(2):
            back(g, side).wait()
        for i, ref in enumerate((dk_ref, dv_ref)):
            ref[g, 0:128, :] = (edge_ref[g % 2, 0, i] + dkv_in[g, 0, i].astype(F32)).astype(BF16)
            ref[g, 896:1024, :] = (edge_ref[g % 2, 1, i] + dkv_in[g, 1, i].astype(F32)).astype(BF16)

    def swap(g):
        return remote(term_ref.at[g, 1 - core], core_in.at[g], core_sem, (g,), sibling)

    def terms(g):
        for t in range(3):
            if t == 0:
                term = nn(ht_ref[...], dq_ref[g])
            else:
                term = nn(xt_ref[...], (dk_ref, dv_ref)[t - 1][g])
            strides = [(256, 64, 16)[axis] for axis in ORDERS[t]]
            for c in range(2):
                for j in range(0, 64, 2):
                    pieces = []
                    for n in (j, j + 1):
                        row = (n // 16) * strides[0] + (n // 4 % 4) * strides[1] + (n % 4) * strides[2] + c * 8
                        pieces.append(term[row:row + 8])
                    term_ref[g, c, t, j * 8:j * 8 + 16, :] = jnp.concatenate(pieces, axis=0).astype(BF16)
        swap(g).start()

    stages = ((a_out, a_in, a_sem, 128), (b_out, b_in, b_sem, 32), (c_out, c_in, c_sem, 8))

    def pass_on(g, level, t, steps):
        out, inside, sem, rows = stages[level]
        axis = ORDERS[t][level]
        first = pl.multiple_of((place[axis] + steps) % 4 * rows, rows)
        return remote(
            out.at[g, t, pl.ds(first, rows), :], inside.at[g, t, steps - 1], sem, (g, t, steps - 1), peer(axis, steps)
        )

    def scatter(g, level):
        for t in range(3):
            for steps in (1, 2, 3):
                pass_on(g, level, t, steps).start()

    def collected(g, level, t):
        out, inside, sem, rows = stages[level]
        for steps in (1, 2, 3):
            pass_on(g, level, t, steps).wait()
        own = pl.ds(pl.multiple_of(place[ORDERS[t][level]] * rows, rows), rows)
        total = out[g, t, own, :].astype(F32)
        for steps in (1, 2, 3):
            total = total + inside[g, t, steps - 1].astype(F32)
        return total

    def reduce_core(g):
        swap(g).wait()
        for t in range(3):
            a_out[g, t] = (term_ref[g, core, t].astype(F32) + core_in[g, t].astype(F32)).astype(BF16)
        scatter(g, 0)

    def reduce_a(g):
        for t in range(3):
            b_out[g, t] = collected(g, 0, t).astype(BF16)
        scatter(g, 1)

    def reduce_b(g):
        for t in range(3):
            c_out[g, t] = collected(g, 1, t)
        scatter(g, 2)

    def reduce_c(g):
        for t in range(3):
            wg_ref[:, pl.ds(pl.multiple_of(t * D + g * W, W), W)] = collected(g, 2, t) * 0.25

    @pl.loop(0, GROUPS)
    def _(g):
        @pl.when(g < GROUPS - 1)
        def _():
            project(g + 1)

        @pl.when(g > 1)
        def _():
            reduce_a(g - 2)

        adjoint(g).wait()
        for side in range(2):
            halo(g, side).wait()
        turn = g % 2
        for i, ref in enumerate((k_ref, v_ref)):
            ref[turn, 0] = kv_in[g, 0, i]
            ref[turn, 9] = kv_in[g, 1, i]

        @pl.loop(0, PAIRS)
        def _(pair):
            @pl.when((pair == 1) & (g > 1))
            def _():
                reduce_b(g - 2)

            @pl.when((pair == 1) & (g > 0))
            def _():
                merge(g - 1)
                terms(g - 1)

            attend_pair(g, pair)

        for side in range(2):
            back(g, side).start()

        @pl.when(g > 1)
        def _():
            reduce_c(g - 2)

        @pl.when(g > 0)
        def _():
            reduce_core(g - 1)

    last = GROUPS - 1
    total = None
    for g in range(GROUPS):
        part = nt(dq_ref[g], w_ref[0, :, g * W:(g + 1) * W])
        total = part if total is None else total + part
    mg_ref[...] = total.astype(BF16)
    pltpu.make_async_copy(mg_ref, mg_hbm, out_sem.at[0]).start()
    reduce_a(last - 1)
    merge(last)
    terms(last)

    def grid_grads(n):
        total = None
        for g in range(GROUPS):
            for i, ref in enumerate((dk_ref, dv_ref)):
                part = nt(ref[g], w_ref[1 + i, n * 256:(n + 1) * 256, g * W:(g + 1) * W])
                total = part if total is None else total + part
        gg_ref[:, n * 256:(n + 1) * 256] = total.astype(BF16)
        grid_out(n).start()

    def grid_out(n):
        return pltpu.make_async_copy(
            gg_ref.at[:, n * 256:(n + 1) * 256], gg_hbm.at[:, n * 256:(n + 1) * 256], out_sem.at[1 + n]
        )

    grid_grads(0)
    reduce_core(last)
    reduce_b(last - 1)
    grid_grads(1)
    reduce_c(last - 1)
    grid_grads(2)
    reduce_a(last)
    grid_grads(3)
    reduce_b(last)
    reduce_c(last)
    copy = pltpu.make_async_copy(wg_ref, wg_hbm, out_sem.at[5])
    copy.start()
    copy.wait()
    pltpu.make_async_copy(mg_ref, mg_hbm, out_sem.at[0]).wait()
    for n in range(4):
        grid_out(n).wait()


def on_device(grid_feat, mesh_feat, mesh_adjoint, w_query, w_key, w_value, block_grid, block_mask):
    anywhere = pl.BlockSpec(memory_space=pl.ANY)
    dma = pltpu.SemaphoreType.DMA
    grid_grad, mesh_grad, w_grad = pl.pallas_call(
        kernel,
        in_specs=[pl.BlockSpec(memory_space=pltpu.SMEM)] + [anywhere] * 7,
        out_specs=[anywhere] * 3,
        out_shape=[
            jax.ShapeDtypeStruct((1024, D), BF16),
            jax.ShapeDtypeStruct((512, D), BF16),
            jax.ShapeDtypeStruct((8, 3 * D), F32),
        ],
        scratch_shapes=[
            pltpu.VMEM((1024, D), BF16),
            pltpu.VMEM((512, D), BF16),
            pltpu.VMEM((D, 1024), BF16),
            pltpu.VMEM((D, 512), BF16),
            pltpu.VMEM((3, D, D), BF16),
            pltpu.VMEM((16, 128, 128), jnp.int32),
            pltpu.VMEM((4, 512, 128), F32),
            pltpu.VMEM((GROUPS, 512, W), BF16),
            pltpu.VMEM((2, 512, W), BF16),
            pltpu.VMEM((2, 10, 128, W), BF16),
            pltpu.VMEM((2, 10, 128, W), BF16),
            pltpu.VMEM((GROUPS, 512, W), BF16),
            pltpu.VMEM((GROUPS, 1024, W), BF16),
            pltpu.VMEM((GROUPS, 1024, W), BF16),
            pltpu.VMEM((17, 128, 128), F32),
            pltpu.VMEM((17, 128, 128), F32),
            pltpu.VMEM((2, 2, 2, 128, W), F32),
            pltpu.VMEM((GROUPS, 2, 2, 128, W), BF16),
            pltpu.VMEM((GROUPS, 2, 2, 128, W), BF16),
            pltpu.VMEM((GROUPS, 2, 2, 128, W), BF16),
            pltpu.VMEM((GROUPS, 2, 2, 128, W), BF16),
            pltpu.VMEM((GROUPS, 2, 3, 512, W), BF16),
            pltpu.VMEM((GROUPS, 3, 512, W), BF16),
            pltpu.VMEM((GROUPS, 3, 512, W), BF16),
            pltpu.VMEM((GROUPS, 3, 3, 128, W), BF16),
            pltpu.VMEM((GROUPS, 3, 128, W), BF16),
            pltpu.VMEM((GROUPS, 3, 3, 32, W), BF16),
            pltpu.VMEM((GROUPS, 3, 32, W), F32),
            pltpu.VMEM((GROUPS, 3, 3, 8, W), F32),
            pltpu.VMEM((8, 3 * D), F32),
            pltpu.VMEM((1024, D), BF16),
            pltpu.VMEM((512, D), BF16),
            pltpu.SMEM((16,), jnp.int32),
            pltpu.SMEM((40,), jnp.int32),
            dma((3,)),
            dma((GROUPS, 3)),
            dma((6,)),
            dma((2, GROUPS)),
            dma((2, GROUPS, 2)),
            dma((2, GROUPS, 2)),
            dma((2, GROUPS)),
            dma((2, GROUPS, 3, 3)),
            dma((2, GROUPS, 3, 3)),
            dma((2, GROUPS, 3, 3)),
        ],
        compiler_params=pltpu.CompilerParams(
            collective_id=0, has_side_effects=True, vmem_limit_bytes=62 << 20
        ),
        cost_estimate=pl.CostEstimate(flops=20 * 2**30, bytes_accessed=20 << 20, transcendentals=4 << 20),
    )(block_grid, grid_feat[0], mesh_feat[0], mesh_adjoint[0], w_query, w_key, w_value, block_mask)
    return (grid_grad[None], mesh_grad[None], w_grad)


def solution(mesh):
    placed = (
        P("sec", "space", None),
        P("sec", "space", None),
        P("sec", "space", None),
        P(),
        P(),
        P(),
        P("space"),
        P("space", None, None),
    )
    return jax.shard_map(
        on_device,
        mesh=mesh,
        in_specs=placed,
        out_specs=(P("sec", "space", None), P("sec", "space", None), P(("sec", "space"), None)),
        check_vma=False,
    )
```

time: 341 us -> 99.2 us (0.29)
  waiting for transfers between devices: 211 us -> 0 us
  Pallas kernels: 33.7 us -> 93.7 us
  starting transfers between devices: 25.6 us -> 0 us
  matrix products: 23.1 us -> 0 us
  other arithmetic: 14.9 us -> 0 us
  between operations: 14.4 us -> 0.65 us
  local copies, waits for them, and re-layouts: 17.8 us -> 4.79 us
    unnamed x2 -> x0, waiting for transfers between devices: 211 us -> none
    pallas_call x1, Pallas kernels: 33.7 us -> 93.7 us  [on_device(): pl.pallas_call(kernel, in_specs=[pl.BlockSpec(memory_space=pltpu.SMEM)] +...]
    ppermute x9 -> x0, starting transfers between devices: 25.5 us -> none  [the longest x4 11 us: passed_along_2(): return lax.ppermute(shard, axis, pairs)]
    dot_general x9 -> x0, matrix products: 23.1 us -> none  [the longest x3 8.5 us: nn(): lax.dot_general(a, b, (((1,), (0,)), ((), ())), preferred_element_type=F32)]
    unnamed x47 -> x7, local copies, waits for them, and re-layouts: 14.8 us -> 4.79 us
    concatenate x2 -> x0, other arithmetic: 6.33 us -> none  [with_halo(): shard = jnp.concatenate([before, shard, after], axis=dim)]
    convert_element_type x1 -> x0, other arithmetic: 4.25 us -> none  [on_device(): terms.astype(BF16)]
    another operation x2 -> x0, other arithmetic: 3.46 us -> none
  transfers between devices with their start and end apart: 10 -> 0, of which waited for: 1 -> 0; matrix products, arithmetic and copies ran while one was open for 9% -> 0% of each run, Pallas kernels for 0% -> 0%
where the time goes in v2:
time: 99.2 us; the launch traced here: 99.1 us
  Pallas kernels  93.7 us (94%)
  local copies, waits for them, and re-layouts  4.79 us (5%)
    pallas_call x1, Pallas kernels, on_device(): pl.pallas_call(kernel, in_specs=[pl.BlockSpec(memory_space=pltpu.SMEM)] +...  93.7 us
    unnamed x7, local copies, waits for them, and re-layouts  4.79 us

profile of v2, /device:TPU:0, one launch (start us, length us, event | category | flops | bytes accessed | tf_op | source)
XLA Modules:
  0.0 99.1 jit_solution(7799688424282708200)
XLA Ops:
  0.6 93.7 %shard_map.103 = (bf16[1024,1024]{1,0:T(8,128)(2,1)}, bf16[512,1024]{1,0:T(8,128)(2,1)}, f32[8,3072]{1,0:T(8,128)}) custom-call(s32[16]{0:T(128)} %ids_ref.1, bf16[1024,1024]{1,0:T(8,128)(2,1)} %bitcast.7, bf16[512,1024]{1,0:T(8,128)(2,1)} %bitcast.8, bf16[512,1024]{1,0:T(8,128)(2,1)} %bitcast.9, bf16[1024,1024]{1,0:T(8,128)(2,1)} %wq_hbm.1, ...), custom_call_target="tpu_custom_call" | custom-call | flops 21474836480 | bytes 20971520 | tf_op jit(solution)/shard_map/pallas_call | solution.py:367
  94.3 0.0 copy-start
  94.3 3.2 %copy.14 = bf16[1,1024,1024]{2,1,0:T(8,128)(2,1)} copy(bf16[1,1024,1024]{2,1,0:T(8,128)(2,1)} %bitcast.5) | data formatting | bytes 4194304
  97.5 0.0 copy-done
  97.5 0.0 copy-start.1
  97.5 1.0 copy.15
  98.5 0.0 copy-done.1
  98.5 0.6 copy.16
Async XLA Ops:
  94.3 3.2 %copy-start = (bf16[512,1024]{1,0:T(8,128)(2,1)S(1)}, bf16[512,1024]{1,0:T(8,128)(2,1)}, u32[]{:S(2)}) copy-start(bf16[512,1024]{1,0:T(8,128)(2,1)} %get-tuple-element.7) | copy-start | bytes 3145732
  97.5 1.0 copy-start.1

commit v3 on v2

--- a/solution.py
+++ b/solution.py
@@ -12,7 +12,7 @@
 W = D // GROUPS
 PAIRS = W // 128
 BANDS = 32
-ORDERS = ((0, 1, 2), (1, 2, 0), (2, 0, 1))
+ORDERS = ((0, 1, 2), (1, 0, 2), (2, 0, 1))
 
 
 def nt(a, b):
@@ -73,7 +73,7 @@
 
     def load_w(g, i):
         return pltpu.make_async_copy(
-            (wq_hbm, wk_hbm, wv_hbm)[i].at[:, cols_of(g)], w_ref.at[i, :, cols_of(g)], w_sem.at[g, i]
+            (wq_hbm, wk_hbm, wv_hbm)[i].at[:, cols_of(g)], w_ref.at[i, g], w_sem.at[g, i]
         )
 
     def remote(src, dst, sem, at, to):
@@ -91,37 +91,41 @@
         load_w(0, i).start()
     load(h_hbm, h_ref, 1).start()
     load_w(0, 0).start()
+    pl.semaphore_wait(barrier, len(peers))
+
+    def adjoint(g):
+        return remote(a_hbm.at[:, cols_of(g)], adj_ref.at[g], adj_sem, (g,), peer(0, 3))
+
+    for g in range(GROUPS):
+        adjoint(g).start()
+
+    def halo(g, side):
+        return remote(kv_out.at[g, side], kv_in.at[g, 1 - side], kv_sem, (g, side), (down, up)[side])
+
+    def project(g):
+        turn = g % 2
+        for i in (1, 2):
+            load_w(g, i).wait()
+            for r in range(4):
+                own = nn(x_ref[r * 256:(r + 1) * 256], w_ref[i, g]).astype(BF16)
+                (k_ref, v_ref)[i - 1][turn, 1 + 2 * r:3 + 2 * r] = own.reshape(2, 128, W)
+                if r == 0:
+                    kv_out[g, 0, i - 1] = own[:128]
+                if r == 3:
+                    kv_out[g, 1, i - 1] = own[128:]
+        for side in range(2):
+            halo(g, side).start()
+        load_w(g, 0).wait()
+        for r in range(2):
+            rows = slice(r * 256, (r + 1) * 256)
+            q_ref[turn, rows] = nn(h_ref[rows], w_ref[0, g]).astype(BF16) * 0.125
+
+    load(x_hbm, x_ref, 0).wait()
+    load(h_hbm, h_ref, 1).wait()
     load(mask_hbm, mask_ref, 2).start()
     for g in range(1, GROUPS):
         for i in range(3):
             load_w(g, i).start()
-    pl.semaphore_wait(barrier, len(peers))
-
-    def adjoint(g):
-        return remote(a_hbm.at[:, cols_of(g)], adj_ref.at[g], adj_sem, (g,), peer(0, 3))
-
-    for g in range(GROUPS):
-        adjoint(g).start()
-
-    def halo(g, side):
-        return remote(kv_out.at[g, side], kv_in.at[g, 1 - side], kv_sem, (g, side), (down, up)[side])
-
-    def project(g):
-        turn = g % 2
-        for i in (1, 2):
-            load_w(g, i).wait()
-            own = nn(x_ref[...], w_ref[i, :, cols_of(g)]).astype(BF16)
-            for b in range(8):
-                (k_ref, v_ref)[i - 1][turn, b + 1] = own[b * 128:(b + 1) * 128]
-            kv_out[g, 0, i - 1] = own[:128]
-            kv_out[g, 1, i - 1] = own[896:]
-        for side in range(2):
-            halo(g, side).start()
-        load_w(g, 0).wait()
-        q_ref[turn] = (nn(h_ref[...], w_ref[0, :, cols_of(g)]).astype(BF16)) * 0.125
-
-    load(x_hbm, x_ref, 0).wait()
-    load(h_hbm, h_ref, 1).wait()
     project(0)
 
     @pl.loop(0, 8)
@@ -215,21 +219,23 @@
     def swap(g):
         return remote(term_ref.at[g, 1 - core], core_in.at[g], core_sem, (g,), sibling)
 
-    def terms(g):
-        for t in range(3):
-            if t == 0:
-                term = nn(ht_ref[...], dq_ref[g])
-            else:
-                term = nn(xt_ref[...], (dk_ref, dv_ref)[t - 1][g])
-            strides = [(256, 64, 16)[axis] for axis in ORDERS[t]]
-            for c in range(2):
-                for j in range(0, 64, 2):
-                    pieces = []
-                    for n in (j, j + 1):
-                        row = (n // 16) * strides[0] + (n // 4 % 4) * strides[1] + (n % 4) * strides[2] + c * 8
-                        pieces.append(term[row:row + 8])
-                    term_ref[g, c, t, j * 8:j * 8 + 16, :] = jnp.concatenate(pieces, axis=0).astype(BF16)
-        swap(g).start()
+    def terms(g, which=(0, 1, 2)):
+        for t in which:
+            strides = [(0, 64, 16)[axis] for axis in ORDERS[t]]
+            for z in range(4):
+                rows = slice(z * 256, (z + 1) * 256)
+                if t == 0:
+                    term = nn(ht_ref[rows], dq_ref[g])
+                else:
+                    term = nn(xt_ref[rows], (dk_ref, dv_ref)[t - 1][g])
+                for c in range(2):
+                    for n in range(0, 64, 2):
+                        at = (n // 16, n // 4 % 4, n % 4)
+                        if at[ORDERS[t].index(0)] != z:
+                            continue
+                        row = sum(a * b for a, b in zip(at, strides)) + c * 8
+                        pieces = [term[row:row + 8], term[row + strides[2]:row + strides[2] + 8]]
+                        term_ref[g, c, t, n * 8:n * 8 + 16, :] = jnp.concatenate(pieces, axis=0).astype(BF16)
 
     stages = ((a_out, a_in, a_sem, 128), (b_out, b_in, b_sem, 32), (c_out, c_in, c_sem, 8))
 
@@ -238,18 +244,21 @@
         axis = ORDERS[t][level]
         first = pl.multiple_of((place[axis] + steps) % 4 * rows, rows)
         return remote(
-            out.at[g, t, pl.ds(first, rows), :], inside.at[g, t, steps - 1], sem, (g, t, steps - 1), peer(axis, steps)
+            out.at[g, t, pl.ds(first, rows), :], inside.at[g, t, steps - 1], sem, (g,), peer(axis, steps)
         )
 
     def scatter(g, level):
-        for t in range(3):
-            for steps in (1, 2, 3):
+        for steps in (2, 1, 3):
+            for t in range(3):
                 pass_on(g, level, t, steps).start()
+
+    def arrived(g, level):
+        _, inside, sem, _ = stages[level]
+        for i in range(2):
+            pltpu.make_async_copy(inside.at[g], inside.at[g], sem.at[i, g]).wait()
 
     def collected(g, level, t):
         out, inside, sem, rows = stages[level]
-        for steps in (1, 2, 3):
-            pass_on(g, level, t, steps).wait()
         own = pl.ds(pl.multiple_of(place[ORDERS[t][level]] * rows, rows), rows)
         total = out[g, t, own, :].astype(F32)
         for steps in (1, 2, 3):
@@ -263,16 +272,19 @@
         scatter(g, 0)
 
     def reduce_a(g):
+        arrived(g, 0)
         for t in range(3):
             b_out[g, t] = collected(g, 0, t).astype(BF16)
         scatter(g, 1)
 
     def reduce_b(g):
+        arrived(g, 1)
         for t in range(3):
             c_out[g, t] = collected(g, 1, t)
         scatter(g, 2)
 
     def reduce_c(g):
+        arrived(g, 2)
         for t in range(3):
             wg_ref[:, pl.ds(pl.multiple_of(t * D + g * W, W), W)] = collected(g, 2, t) * 0.25
 
@@ -281,10 +293,6 @@
         @pl.when(g < GROUPS - 1)
         def _():
             project(g + 1)
-
-        @pl.when(g > 1)
-        def _():
-            reduce_a(g - 2)
 
         adjoint(g).wait()
         for side in range(2):
@@ -296,14 +304,19 @@
 
         @pl.loop(0, PAIRS)
         def _(pair):
+            @pl.when((pair == 1) & (g > 2))
+            def _():
+                reduce_c(g - 3)
+
             @pl.when((pair == 1) & (g > 1))
             def _():
-                reduce_b(g - 2)
+                reduce_a(g - 2)
 
             @pl.when((pair == 1) & (g > 0))
             def _():
                 merge(g - 1)
                 terms(g - 1)
+                swap(g - 1).start()
 
             attend_pair(g, pair)
 
@@ -312,30 +325,38 @@
 
         @pl.when(g > 1)
         def _():
-            reduce_c(g - 2)
+            reduce_b(g - 2)
 
         @pl.when(g > 0)
         def _():
             reduce_core(g - 1)
 
     last = GROUPS - 1
-    total = None
-    for g in range(GROUPS):
-        part = nt(dq_ref[g], w_ref[0, :, g * W:(g + 1) * W])
-        total = part if total is None else total + part
-    mg_ref[...] = total.astype(BF16)
+    terms(last, (0,))
+    for r in range(2):
+        rows = slice(r * 256, (r + 1) * 256)
+        for n in range(4):
+            cols = slice(n * 256, (n + 1) * 256)
+            total = None
+            for g in range(GROUPS):
+                part = nt(dq_ref[g, rows], w_ref[0, g, cols])
+                total = part if total is None else total + part
+            mg_ref[rows, cols] = total.astype(BF16)
     pltpu.make_async_copy(mg_ref, mg_hbm, out_sem.at[0]).start()
-    reduce_a(last - 1)
     merge(last)
-    terms(last)
+    terms(last, (1, 2))
+    swap(last).start()
 
     def grid_grads(n):
-        total = None
-        for g in range(GROUPS):
-            for i, ref in enumerate((dk_ref, dv_ref)):
-                part = nt(ref[g], w_ref[1 + i, n * 256:(n + 1) * 256, g * W:(g + 1) * W])
-                total = part if total is None else total + part
-        gg_ref[:, n * 256:(n + 1) * 256] = total.astype(BF16)
+        cols = slice(n * 256, (n + 1) * 256)
+        for r in range(4):
+            rows = slice(r * 256, (r + 1) * 256)
+            total = None
+            for g in range(GROUPS):
+                for i, ref in enumerate((dk_ref, dv_ref)):
+                    part = nt(ref[g, rows], w_ref[1 + i, g, cols])
+                    total = part if total is None else total + part
+            gg_ref[rows, cols] = total.astype(BF16)
         grid_out(n).start()
 
     def grid_out(n):
@@ -344,13 +365,15 @@
         )
 
     grid_grads(0)
+    reduce_a(last - 1)
+    grid_grads(1)
     reduce_core(last)
+    reduce_c(last - 2)
     reduce_b(last - 1)
-    grid_grads(1)
+    grid_grads(2)
+    grid_grads(3)
+    reduce_a(last)
     reduce_c(last - 1)
-    grid_grads(2)
-    reduce_a(last)
-    grid_grads(3)
     reduce_b(last)
     reduce_c(last)
     copy = pltpu.make_async_copy(wg_ref, wg_hbm, out_sem.at[5])
@@ -359,6 +382,26 @@
     pltpu.make_async_copy(mg_ref, mg_hbm, out_sem.at[0]).wait()
     for n in range(4):
         grid_out(n).wait()
+
+
+def hand_out(gg, mg, wg, gg_out, mg_out, wg_out, gg_ref, mg_ref, wg_ref, sem):
+    steps = []
+    for src, held, dst, parts in ((gg, gg_ref, gg_out, 4), (mg, mg_ref, mg_out, 2), (wg, wg_ref, wg_out, 1)):
+        rows = src.shape[0] // parts
+        for part in range(parts):
+            at = pl.ds(part * rows, rows)
+            n = len(steps)
+            steps.append((
+                pltpu.make_async_copy(src.at[at], held.at[at], sem.at[0, n]),
+                pltpu.make_async_copy(held.at[at], dst.at[at], sem.at[1, n]),
+            ))
+    for come, _ in steps:
+        come.start()
+    for come, go in steps:
+        come.wait()
+        go.start()
+    for _, go in steps:
+        go.wait()
 
 
 def on_device(grid_feat, mesh_feat, mesh_adjoint, w_query, w_key, w_value, block_grid, block_mask):
@@ -378,7 +421,7 @@
             pltpu.VMEM((512, D), BF16),
             pltpu.VMEM((D, 1024), BF16),
             pltpu.VMEM((D, 512), BF16),
-            pltpu.VMEM((3, D, D), BF16),
+            pltpu.VMEM((3, GROUPS, D, W), BF16),
             pltpu.VMEM((16, 128, 128), jnp.int32),
             pltpu.VMEM((4, 512, 128), F32),
             pltpu.VMEM((GROUPS, 512, W), BF16),
@@ -415,15 +458,23 @@
             dma((2, GROUPS, 2)),
             dma((2, GROUPS, 2)),
             dma((2, GROUPS)),
-            dma((2, GROUPS, 3, 3)),
-            dma((2, GROUPS, 3, 3)),
-            dma((2, GROUPS, 3, 3)),
+            dma((2, GROUPS)),
+            dma((2, GROUPS)),
+            dma((2, GROUPS)),
         ],
         compiler_params=pltpu.CompilerParams(
             collective_id=0, has_side_effects=True, vmem_limit_bytes=62 << 20
         ),
         cost_estimate=pl.CostEstimate(flops=20 * 2**30, bytes_accessed=20 << 20, transcendentals=4 << 20),
     )(block_grid, grid_feat[0], mesh_feat[0], mesh_adjoint[0], w_query, w_key, w_value, block_mask)
+    results = (grid_grad, mesh_grad, w_grad)
+    grid_grad, mesh_grad, w_grad = pl.pallas_call(
+        hand_out,
+        in_specs=[anywhere] * 3,
+        out_specs=[anywhere] * 3,
+        out_shape=[jax.ShapeDtypeStruct(r.shape, r.dtype) for r in results],
+        scratch_shapes=[pltpu.VMEM(r.shape, r.dtype) for r in results] + [dma((2, 7))],
+    )(*results)
     return (grid_grad[None], mesh_grad[None], w_grad)
 
 

time: 99.2 us -> 83.3 us (0.84)
  Pallas kernels: 93.7 us -> 82.6 us
  local copies, waits for them, and re-layouts: 4.79 us -> 0 us
    pallas_call x1, Pallas kernels: 93.7 us -> 79.7 us  [on_device(): pl.pallas_call(kernel, in_specs=[pl.BlockSpec(memory_space=pltpu.SMEM)] +...]
    unnamed x7 -> x0, local copies, waits for them, and re-layouts: 4.79 us -> none
    pallas_call x0 -> x1, Pallas kernels: none -> 2.84 us  [on_device(): pl.pallas_call(hand_out, in_specs=[anywhere] * 3, out_specs=[anywhere] *...]
where the time goes in v3:
time: 83.3 us; the launch traced here: 83.2 us
  Pallas kernels  82.6 us (99%)
    pallas_call x1, Pallas kernels, on_device(): pl.pallas_call(kernel, in_specs=[pl.BlockSpec(memory_space=pltpu.SMEM)] +...  79.7 us
    pallas_call x1, Pallas kernels, on_device(): pl.pallas_call(hand_out, in_specs=[anywhere] * 3, out_specs=[anywhere] *...  2.84 us

profile of v3, /device:TPU:0, one launch (start us, length us, event | category | flops | bytes accessed | tf_op | source)
XLA Modules:
  0.0 83.2 jit_solution(15340023733364618431)
XLA Ops:
  0.6 79.7 %shard_map.103 = (bf16[1024,1024]{1,0:T(8,128)(2,1)}, bf16[512,1024]{1,0:T(8,128)(2,1)}, f32[8,3072]{1,0:T(8,128)}) custom-call(s32[16]{0:T(128)} %ids_ref.1, bf16[1024,1024]{1,0:T(8,128)(2,1)} %bitcast.5, bf16[512,1024]{1,0:T(8,128)(2,1)} %bitcast.7, bf16[512,1024]{1,0:T(8,128)(2,1)} %bitcast.8, bf16[1024,1024]{1,0:T(8,128)(2,1)} %wq_hbm.1, ...), custom_call_target="tpu_custom_call" | custom-call | flops 21474836480 | bytes 20971520 | tf_op jit(solution)/shard_map/pallas_call | solution.py:410
  80.4 2.8 %shard_map.104 = (bf16[1024,1024]{1,0:T(8,128)(2,1)}, bf16[512,1024]{1,0:T(8,128)(2,1)}, f32[8,3072]{1,0:T(8,128)}) custom-call(bf16[1024,1024]{1,0:T(8,128)(2,1)} %get-tuple-element.9.gg, bf16[512,1024]{1,0:T(8,128)(2,1)} %get-tuple-element.10.mg, f32[8,3072]{1,0:T(8,128)} %get-tuple-element.11.wg), custom_call_target="tpu_custom_call" | custom-call | tf_op jit(solution)/shard_map/pallas_call | solution.py:471

commit v4 on v3

--- a/solution.py
+++ b/solution.py
@@ -60,6 +60,8 @@
             return (z, space_of((x + steps) % 4, y, core))
         return (z, space_of(x, (y + steps) % 4, core))
 
+    near = {(axis, steps): peer(axis, steps) for axis in range(3) for steps in (1, 2, 3)}
+    ahead = {(axis, steps): (place[axis] + steps) % 4 for axis in range(3) for steps in (1, 2, 3)}
     sibling = (sec, space_of(gx, gy, 1 - core))
     up = (sec, (band + 1) % BANDS)
     down = (sec, (band + BANDS - 1) % BANDS)
@@ -83,7 +85,7 @@
         )
 
     barrier = pltpu.get_barrier_semaphore()
-    peers = [sibling, across] + [peer(axis, steps) for axis in range(3) for steps in (1, 2, 3)]
+    peers = [sibling, across] + [*near.values()]
     for to in peers:
         pl.semaphore_signal(barrier, inc=1, device_id=to, device_id_type=MESH)
     load(x_hbm, x_ref, 0).start()
@@ -94,10 +96,9 @@
     pl.semaphore_wait(barrier, len(peers))
 
     def adjoint(g):
-        return remote(a_hbm.at[:, cols_of(g)], adj_ref.at[g], adj_sem, (g,), peer(0, 3))
-
-    for g in range(GROUPS):
-        adjoint(g).start()
+        return remote(a_hbm.at[:, cols_of(g)], adj_ref.at[g], adj_sem, (g,), near[0, 3])
+
+    adjoint(0).start()
 
     def halo(g, side):
         return remote(kv_out.at[g, side], kv_in.at[g, 1 - side], kv_sem, (g, side), (down, up)[side])
@@ -158,7 +159,7 @@
                 at = at + (1 - jnp.minimum(off * off, 1)) * (m * 4 + s - 16)
             lists_ref[block * 4 + m] = jnp.clip(at, 0, 16)
 
-    def attend(g, pair, m):
+    def operands(g, pair, m):
         turn = g % 2
         rows = slice(m * 128, (m + 1) * 128)
         cols = pl.ds(pl.multiple_of(pair * 128, 128), 128)
@@ -167,16 +168,22 @@
         values = jnp.concatenate([v_ref[turn, b, :, cols] for b in blocks], axis=0)
         qq = paired(q_ref[turn, rows, cols])
         aa = paired(adj_ref[g, rows, cols])
+        return keys, qq, aa, nt(keys, qq), nt(values, aa)
+
+    def weigh(m, scores, dprobs):
         bias = bias_ref[m]
         bias = jnp.concatenate([bias, bias], axis=1)
-        scores = nt(keys, qq) + bias
+        scores = scores + bias
         top = jnp.max(scores, axis=0, keepdims=True)
         expo = jnp.exp(scores - top)
         probs = expo * (1.0 / jnp.sum(expo, axis=0, keepdims=True))
         probs_b = probs.astype(BF16)
-        dprobs = nt(values, aa)
         delta = jnp.sum(probs_b.astype(F32) * dprobs, axis=0, keepdims=True)
-        ds = (probs * (dprobs - delta)).astype(BF16)
+        return probs_b, (probs * (dprobs - delta)).astype(BF16)
+
+    def spread(g, pair, m, keys, qq, aa, probs_b, ds):
+        rows = slice(m * 128, (m + 1) * 128)
+        cols = pl.ds(pl.multiple_of(pair * 128, 128), 128)
         dv = nn(probs_b, aa)
         dk = nn(ds, qq)
         for s in range(4):
@@ -192,8 +199,17 @@
 
     def attend_pair(g, pair):
         cols = pl.ds(pl.multiple_of(pair * 128, 128), 128)
+        ready = operands(g, pair, 0)
+        done = None
         for m in range(4):
-            attend(g, pair, m)
+            keys, qq, aa, scores, dprobs = ready
+            if m < 3:
+                ready = operands(g, pair, m + 1)
+            weighed = weigh(m, scores, dprobs)
+            if done is not None:
+                spread(g, pair, m - 1, *done)
+            done = (keys, qq, aa, *weighed)
+        spread(g, pair, 3, *done)
         for i, part in enumerate((dk_part, dv_part)):
             dkv_out[g, 0, i, :, cols] = gathered(part, 0).astype(BF16)
             dkv_out[g, 1, i, :, cols] = gathered(part, 9).astype(BF16)
@@ -239,18 +255,22 @@
 
     stages = ((a_out, a_in, a_sem, 128), (b_out, b_in, b_sem, 32), (c_out, c_in, c_sem, 8))
 
-    def pass_on(g, level, t, steps):
+    bundles = (((0, 1), (1, 2), (2, 3)), ((0, 1), (1, 3)), ((0, 2), (2, 3)))
+
+    def pass_on(g, level, bundle, steps):
         out, inside, sem, rows = stages[level]
-        axis = ORDERS[t][level]
-        first = pl.multiple_of((place[axis] + steps) % 4 * rows, rows)
+        axis = ORDERS[bundle[0]][level]
+        both = pl.ds(bundle[0], bundle[1] - bundle[0])
+        first = pl.multiple_of(ahead[axis, steps] * rows, rows)
         return remote(
-            out.at[g, t, pl.ds(first, rows), :], inside.at[g, t, steps - 1], sem, (g,), peer(axis, steps)
+            out.at[g, both, pl.ds(first, rows), :], inside.at[g, steps - 1, both], sem, (g,), near[axis, steps]
         )
 
-    def scatter(g, level):
+    def scatter(g, level, which=(0, 1, 2)):
         for steps in (2, 1, 3):
-            for t in range(3):
-                pass_on(g, level, t, steps).start()
+            for n, bundle in enumerate(bundles[level]):
+                if n in which:
+                    pass_on(g, level, bundle, steps).start()
 
     def arrived(g, level):
         _, inside, sem, _ = stages[level]
@@ -262,14 +282,27 @@
         own = pl.ds(pl.multiple_of(place[ORDERS[t][level]] * rows, rows), rows)
         total = out[g, t, own, :].astype(F32)
         for steps in (1, 2, 3):
-            total = total + inside[g, t, steps - 1].astype(F32)
+            total = total + inside[g, steps - 1, t].astype(F32)
         return total
+
+    def join_core(g, t):
+        a_out[g, t] = (term_ref[g, core, t].astype(F32) + core_in[g, t].astype(F32)).astype(BF16)
 
     def reduce_core(g):
         swap(g).wait()
         for t in range(3):
-            a_out[g, t] = (term_ref[g, core, t].astype(F32) + core_in[g, t].astype(F32)).astype(BF16)
+            join_core(g, t)
         scatter(g, 0)
+
+    def swap_one(t):
+        return remote(
+            term_ref.at[GROUPS - 1, 1 - core, t], core_in.at[GROUPS - 1, t], core_sem, (GROUPS - 1 + t,), sibling
+        )
+
+    def reduce_core_one(t):
+        swap_one(t).wait()
+        join_core(GROUPS - 1, t)
+        scatter(GROUPS - 1, 0, (t,))
 
     def reduce_a(g):
         arrived(g, 0)
@@ -295,6 +328,11 @@
             project(g + 1)
 
         adjoint(g).wait()
+
+        @pl.when(g < GROUPS - 1)
+        def _():
+            adjoint(g + 1).start()
+
         for side in range(2):
             halo(g, side).wait()
         turn = g % 2
@@ -333,6 +371,7 @@
 
     last = GROUPS - 1
     terms(last, (0,))
+    swap_one(0).start()
     for r in range(2):
         rows = slice(r * 256, (r + 1) * 256)
         for n in range(4):
@@ -344,8 +383,9 @@
             mg_ref[rows, cols] = total.astype(BF16)
     pltpu.make_async_copy(mg_ref, mg_hbm, out_sem.at[0]).start()
     merge(last)
-    terms(last, (1, 2))
-    swap(last).start()
+    for t in (1, 2):
+        terms(last, (t,))
+        swap_one(t).start()
 
     def grid_grads(n):
         cols = slice(n * 256, (n + 1) * 256)
@@ -364,10 +404,12 @@
             gg_ref.at[:, n * 256:(n + 1) * 256], gg_hbm.at[:, n * 256:(n + 1) * 256], out_sem.at[1 + n]
         )
 
+    reduce_core_one(0)
     grid_grads(0)
+    reduce_core_one(1)
     reduce_a(last - 1)
+    reduce_core_one(2)
     grid_grads(1)
-    reduce_core(last)
     reduce_c(last - 2)
     reduce_b(last - 1)
     grid_grads(2)
@@ -457,7 +499,7 @@
             dma((2, GROUPS)),
             dma((2, GROUPS, 2)),
             dma((2, GROUPS, 2)),
-            dma((2, GROUPS)),
+            dma((2, GROUPS + 2)),
             dma((2, GROUPS)),
             dma((2, GROUPS)),
             dma((2, GROUPS)),

time: 83.3 us -> 80.8 us (0.970)
  Pallas kernels: 82.6 us -> 80 us
    pallas_call x1, Pallas kernels: 79.7 us -> 77.1 us  [on_device(): pl.pallas_call(kernel, in_specs=[pl.BlockSpec(memory_space=pltpu.SMEM)] +...]
where the time goes in v4:
time: 80.8 us; the launch traced here: 80.6 us
  Pallas kernels  80 us (99%)
    pallas_call x1, Pallas kernels, on_device(): pl.pallas_call(kernel, in_specs=[pl.BlockSpec(memory_space=pltpu.SMEM)] +...  77.1 us
    pallas_call x1, Pallas kernels, on_device(): pl.pallas_call(hand_out, in_specs=[anywhere] * 3, out_specs=[anywhere] *...  2.84 us

profile of v4, /device:TPU:0, one launch (start us, length us, event | category | flops | bytes accessed | tf_op | source)
XLA Modules:
  0.0 80.6 jit_solution(11951469513425778782)
XLA Ops:
  0.6 77.1 %shard_map.103 = (bf16[1024,1024]{1,0:T(8,128)(2,1)}, bf16[512,1024]{1,0:T(8,128)(2,1)}, f32[8,3072]{1,0:T(8,128)}) custom-call(s32[16]{0:T(128)} %ids_ref.1, bf16[1024,1024]{1,0:T(8,128)(2,1)} %bitcast.5, bf16[512,1024]{1,0:T(8,128)(2,1)} %bitcast.7, bf16[512,1024]{1,0:T(8,128)(2,1)} %bitcast.8, bf16[1024,1024]{1,0:T(8,128)(2,1)} %wq_hbm.1, ...), custom_call_target="tpu_custom_call" | custom-call | flops 21474836480 | bytes 20971520 | tf_op jit(solution)/shard_map/pallas_call | solution.py:452
  77.8 2.8 %shard_map.104 = (bf16[1024,1024]{1,0:T(8,128)(2,1)}, bf16[512,1024]{1,0:T(8,128)(2,1)}, f32[8,3072]{1,0:T(8,128)}) custom-call(bf16[1024,1024]{1,0:T(8,128)(2,1)} %get-tuple-element.9.gg, bf16[512,1024]{1,0:T(8,128)(2,1)} %get-tuple-element.10.mg, f32[8,3072]{1,0:T(8,128)} %get-tuple-element.11.wg), custom_call_target="tpu_custom_call" | custom-call | tf_op jit(solution)/shard_map/pallas_call | solution.py:513

commit v5 on v4

--- a/solution.py
+++ b/solution.py
@@ -40,7 +40,7 @@
     dq_ref, dk_ref, dv_ref, dk_part, dv_part, edge_ref,
     kv_out, kv_in, dkv_out, dkv_in,
     term_ref, core_in, a_out, a_in, b_out, b_in, c_out, c_in, wg_ref, gg_ref, mg_ref,
-    local_ref, lists_ref, load_sem, w_sem, out_sem, adj_sem, kv_sem, dkv_sem, core_sem, a_sem, b_sem, c_sem,
+    xh_ref, xht_ref, xh_sem, local_ref, lists_ref, load_sem, w_sem, out_sem, adj_sem, kv_sem, dkv_sem, core_sem, a_sem, b_sem, c_sem,
 ):
     sec = lax.axis_index("sec")
     band = lax.axis_index("space")
@@ -86,13 +86,19 @@
 
     barrier = pltpu.get_barrier_semaphore()
     peers = [sibling, across] + [*near.values()]
+    def load_x(r):
+        rows = slice(r * 256, (r + 1) * 256)
+        return load(x_hbm.at[rows], x_ref.at[rows], 3 + r)
+
+    load_x(0).start()
+    for i in (1, 2):
+        load_w(0, i).start()
+    for r in (3, 1, 2):
+        load_x(r).start()
+    load(h_hbm, h_ref, 1).start()
+    load_w(0, 0).start()
     for to in peers:
         pl.semaphore_signal(barrier, inc=1, device_id=to, device_id_type=MESH)
-    load(x_hbm, x_ref, 0).start()
-    for i in (1, 2):
-        load_w(0, i).start()
-    load(h_hbm, h_ref, 1).start()
-    load_w(0, 0).start()
     pl.semaphore_wait(barrier, len(peers))
 
     def adjoint(g):
@@ -103,41 +109,55 @@
     def halo(g, side):
         return remote(kv_out.at[g, side], kv_in.at[g, 1 - side], kv_sem, (g, side), (down, up)[side])
 
+    def project_kv(g, i, r):
+        own = nn(x_ref[r * 256:(r + 1) * 256], w_ref[i, g]).astype(BF16)
+        (k_ref, v_ref)[i - 1][g % 2, 1 + 2 * r:3 + 2 * r] = own.reshape(2, 128, W)
+        if r == 0:
+            kv_out[g, 0, i - 1] = own[:128]
+        if r == 3:
+            kv_out[g, 1, i - 1] = own[128:]
+
+    def project_q(g):
+        load_w(g, 0).wait()
+        for r in range(2):
+            rows = slice(r * 256, (r + 1) * 256)
+            q_ref[g % 2, rows] = nn(h_ref[rows], w_ref[0, g]).astype(BF16) * 0.125
+
+    def points(side):
+        rows = pl.ds(896 * side, 128)
+        return remote(x_hbm.at[rows], xh_ref.at[1 - side], xh_sem, (side,), (down, up)[side])
+
+    def send_halos(g):
+        for side in range(2):
+            halo(g, side).start()
+
     def project(g):
-        turn = g % 2
         for i in (1, 2):
             load_w(g, i).wait()
             for r in range(4):
-                own = nn(x_ref[r * 256:(r + 1) * 256], w_ref[i, g]).astype(BF16)
-                (k_ref, v_ref)[i - 1][turn, 1 + 2 * r:3 + 2 * r] = own.reshape(2, 128, W)
-                if r == 0:
-                    kv_out[g, 0, i - 1] = own[:128]
-                if r == 3:
-                    kv_out[g, 1, i - 1] = own[128:]
-        for side in range(2):
-            halo(g, side).start()
-        load_w(g, 0).wait()
-        for r in range(2):
-            rows = slice(r * 256, (r + 1) * 256)
-            q_ref[turn, rows] = nn(h_ref[rows], w_ref[0, g]).astype(BF16) * 0.125
-
-    load(x_hbm, x_ref, 0).wait()
+                project_kv(g, i, r)
+        send_halos(g)
+        project_q(g)
+
+    for r in (0, 3, 1, 2):
+        load_x(r).wait()
+        for i in (1, 2):
+            if r == 0:
+                load_w(0, i).wait()
+            project_kv(0, i, r)
+        rows = slice(r * 256, (r + 1) * 256)
+        xt_ref[:, rows] = x_ref[rows].T
+        if r == 3:
+            send_halos(0)
+            load(mask_hbm, mask_ref, 2).start()
+            for g in range(1, GROUPS):
+                for i in range(3):
+                    load_w(g, i).start()
     load(h_hbm, h_ref, 1).wait()
-    load(mask_hbm, mask_ref, 2).start()
-    for g in range(1, GROUPS):
-        for i in range(3):
-            load_w(g, i).start()
-    project(0)
-
-    @pl.loop(0, 8)
-    def _(i):
-        rows = pl.ds(pl.multiple_of(i * 128, 128), 128)
-        xt_ref[:, rows] = x_ref[rows, :].T
-
-    @pl.loop(0, 4)
-    def _(i):
-        rows = pl.ds(pl.multiple_of(i * 128, 128), 128)
-        ht_ref[:, rows] = h_ref[rows, :].T
+    project_q(0)
+    for r in range(2):
+        rows = slice(r * 256, (r + 1) * 256)
+        ht_ref[:, rows] = h_ref[rows].T
 
     load(mask_hbm, mask_ref, 2).wait()
 
@@ -216,6 +236,11 @@
             edge_ref[g % 2, 0, i, :, cols] = gathered(part, 1)
             edge_ref[g % 2, 1, i, :, cols] = gathered(part, 8)
 
+        @pl.when(pair == PAIRS - 1)
+        def _():
+            for side in range(2):
+                back(g, side).start()
+
         @pl.loop(1, 7)
         def _(block):
             rows = pl.ds(pl.multiple_of(block * 128, 128), 128)
@@ -235,7 +260,7 @@
     def swap(g):
         return remote(term_ref.at[g, 1 - core], core_in.at[g], core_sem, (g,), sibling)
 
-    def terms(g, which=(0, 1, 2)):
+    def terms(g, which=(0, 1, 2), outside=False):
         for t in which:
             strides = [(0, 64, 16)[axis] for axis in ORDERS[t]]
             for z in range(4):
@@ -244,6 +269,9 @@
                     term = nn(ht_ref[rows], dq_ref[g])
                 else:
                     term = nn(xt_ref[rows], (dk_ref, dv_ref)[t - 1][g])
+                    if outside:
+                        beyond = jnp.concatenate([dkv_out[g, 0, t - 1], dkv_out[g, 1, t - 1]], axis=0)
+                        term = term + nn(xht_ref[rows], beyond)
                 for c in range(2):
                     for n in range(0, 64, 2):
                         at = (n // 16, n // 4 % 4, n % 4)
@@ -335,6 +363,18 @@
 
         for side in range(2):
             halo(g, side).wait()
+        @pl.when(g == 0)
+        def _():
+            for side in range(2):
+                points(side).start()
+
+        @pl.when(g == GROUPS - 2)
+        def _():
+            for side in range(2):
+                points(side).wait()
+            for side in range(2):
+                xht_ref[:, side * 128:(side + 1) * 128] = xh_ref[side].T
+
         turn = g % 2
         for i, ref in enumerate((k_ref, v_ref)):
             ref[turn, 0] = kv_in[g, 0, i]
@@ -358,9 +398,6 @@
 
             attend_pair(g, pair)
 
-        for side in range(2):
-            back(g, side).start()
-
         @pl.when(g > 1)
         def _():
             reduce_b(g - 2)
@@ -370,8 +407,12 @@
             reduce_core(g - 1)
 
     last = GROUPS - 1
-    terms(last, (0,))
-    swap_one(0).start()
+    for i, ref in enumerate((dk_ref, dv_ref)):
+        ref[last, 0:128, :] = edge_ref[last % 2, 0, i].astype(BF16)
+        ref[last, 896:1024, :] = edge_ref[last % 2, 1, i].astype(BF16)
+    for t in range(3):
+        terms(last, (t,), t > 0)
+        swap_one(t).start()
     for r in range(2):
         rows = slice(r * 256, (r + 1) * 256)
         for n in range(4):
@@ -382,10 +423,6 @@
                 total = part if total is None else total + part
             mg_ref[rows, cols] = total.astype(BF16)
     pltpu.make_async_copy(mg_ref, mg_hbm, out_sem.at[0]).start()
-    merge(last)
-    for t in (1, 2):
-        terms(last, (t,))
-        swap_one(t).start()
 
     def grid_grads(n):
         cols = slice(n * 256, (n + 1) * 256)
@@ -405,10 +442,11 @@
         )
 
     reduce_core_one(0)
+    reduce_core_one(1)
+    merge(last)
+    reduce_core_one(2)
+    reduce_a(last - 1)
     grid_grads(0)
-    reduce_core_one(1)
-    reduce_a(last - 1)
-    reduce_core_one(2)
     grid_grads(1)
     reduce_c(last - 2)
     reduce_b(last - 1)
@@ -491,9 +529,12 @@
             pltpu.VMEM((8, 3 * D), F32),
             pltpu.VMEM((1024, D), BF16),
             pltpu.VMEM((512, D), BF16),
+            pltpu.VMEM((2, 128, D), BF16),
+            pltpu.VMEM((D, 256), BF16),
+            dma((2, 2)),
             pltpu.SMEM((16,), jnp.int32),
             pltpu.SMEM((40,), jnp.int32),
-            dma((3,)),
+            dma((7,)),
             dma((GROUPS, 3)),
             dma((6,)),
             dma((2, GROUPS)),

time: 80.8 us -> 78.3 us (0.969)
  Pallas kernels: 80 us -> 77.5 us
    pallas_call x1, Pallas kernels: 77.1 us -> 74.7 us  [on_device(): pl.pallas_call(kernel, in_specs=[pl.BlockSpec(memory_space=pltpu.SMEM)] +...]
where the time goes in v5:
time: 78.3 us; the launch traced here: 78.1 us
  Pallas kernels  77.5 us (99%)
    pallas_call x1, Pallas kernels, on_device(): pl.pallas_call(kernel, in_specs=[pl.BlockSpec(memory_space=pltpu.SMEM)] +...  74.7 us
    pallas_call x1, Pallas kernels, on_device(): pl.pallas_call(hand_out, in_specs=[anywhere] * 3, out_specs=[anywhere] *...  2.84 us

profile of v5, /device:TPU:0, one launch (start us, length us, event | category | flops | bytes accessed | tf_op | source)
XLA Modules:
  0.0 78.1 jit_solution(13524561873241102365)
XLA Ops:
  0.6 74.7 %shard_map.103 = (bf16[1024,1024]{1,0:T(8,128)(2,1)}, bf16[512,1024]{1,0:T(8,128)(2,1)}, f32[8,3072]{1,0:T(8,128)}) custom-call(s32[16]{0:T(128)} %ids_ref.1, bf16[1024,1024]{1,0:T(8,128)(2,1)} %bitcast.5, bf16[512,1024]{1,0:T(8,128)(2,1)} %bitcast.7, bf16[512,1024]{1,0:T(8,128)(2,1)} %bitcast.8, bf16[1024,1024]{1,0:T(8,128)(2,1)} %wq_hbm.1, ...), custom_call_target="tpu_custom_call" | custom-call | flops 21474836480 | bytes 20971520 | tf_op jit(solution)/shard_map/pallas_call | solution.py:490
  75.3 2.8 %shard_map.104 = (bf16[1024,1024]{1,0:T(8,128)(2,1)}, bf16[512,1024]{1,0:T(8,128)(2,1)}, f32[8,3072]{1,0:T(8,128)}) custom-call(bf16[1024,1024]{1,0:T(8,128)(2,1)} %get-tuple-element.9.gg, bf16[512,1024]{1,0:T(8,128)(2,1)} %get-tuple-element.10.mg, f32[8,3072]{1,0:T(8,128)} %get-tuple-element.11.wg), custom_call_target="tpu_custom_call" | custom-call | tf_op jit(solution)/shard_map/pallas_call | solution.py:554

commit v6 on v5

--- a/solution.py
+++ b/solution.py
@@ -105,6 +105,16 @@
         return remote(a_hbm.at[:, cols_of(g)], adj_ref.at[g], adj_sem, (g,), near[0, 3])
 
     adjoint(0).start()
+
+    for e in range(16):
+        local_ref[e] = jnp.clip(ids_ref[e] - band * 8 + 1, 0, 9)
+    for block in range(10):
+        for m in range(4):
+            at = 16
+            for s in range(4):
+                off = local_ref[m * 4 + s] - block
+                at = at + (1 - jnp.minimum(off * off, 1)) * (m * 4 + s - 16)
+            lists_ref[block * 4 + m] = jnp.clip(at, 0, 16)
 
     def halo(g, side):
         return remote(kv_out.at[g, side], kv_in.at[g, 1 - side], kv_sem, (g, side), (down, up)[side])
@@ -169,15 +179,6 @@
     dk_part[16] = jnp.zeros((128, 128), F32)
     dv_part[16] = jnp.zeros((128, 128), F32)
 
-    for e in range(16):
-        local_ref[e] = jnp.clip(ids_ref[e] - band * 8 + 1, 0, 9)
-    for block in range(10):
-        for m in range(4):
-            at = 16
-            for s in range(4):
-                off = local_ref[m * 4 + s] - block
-                at = at + (1 - jnp.minimum(off * off, 1)) * (m * 4 + s - 16)
-            lists_ref[block * 4 + m] = jnp.clip(at, 0, 16)
 
     def operands(g, pair, m):
         turn = g % 2
@@ -257,8 +258,8 @@
             ref[g, 0:128, :] = (edge_ref[g % 2, 0, i] + dkv_in[g, 0, i].astype(F32)).astype(BF16)
             ref[g, 896:1024, :] = (edge_ref[g % 2, 1, i] + dkv_in[g, 1, i].astype(F32)).astype(BF16)
 
-    def swap(g):
-        return remote(term_ref.at[g, 1 - core], core_in.at[g], core_sem, (g,), sibling)
+    def swap(g, t):
+        return remote(term_ref.at[g, 1 - core, t], core_in.at[g, t], core_sem, (g, t), sibling)
 
     def terms(g, which=(0, 1, 2), outside=False):
         for t in which:
@@ -316,21 +317,11 @@
     def join_core(g, t):
         a_out[g, t] = (term_ref[g, core, t].astype(F32) + core_in[g, t].astype(F32)).astype(BF16)
 
-    def reduce_core(g):
-        swap(g).wait()
-        for t in range(3):
+    def reduce_core(g, which=(0, 1, 2)):
+        for t in which:
+            swap(g, t).wait()
             join_core(g, t)
-        scatter(g, 0)
-
-    def swap_one(t):
-        return remote(
-            term_ref.at[GROUPS - 1, 1 - core, t], core_in.at[GROUPS - 1, t], core_sem, (GROUPS - 1 + t,), sibling
-        )
-
-    def reduce_core_one(t):
-        swap_one(t).wait()
-        join_core(GROUPS - 1, t)
-        scatter(GROUPS - 1, 0, (t,))
+        scatter(g, 0, which)
 
     def reduce_a(g):
         arrived(g, 0)
@@ -382,19 +373,20 @@
 
         @pl.loop(0, PAIRS)
         def _(pair):
+            @pl.when((pair == 1) & (g > 0))
+            def _():
+                merge(g - 1)
+                for t in range(3):
+                    terms(g - 1, (t,))
+                    swap(g - 1, t).start()
+
+            @pl.when((pair == 1) & (g > 1))
+            def _():
+                reduce_a(g - 2)
+
             @pl.when((pair == 1) & (g > 2))
             def _():
                 reduce_c(g - 3)
-
-            @pl.when((pair == 1) & (g > 1))
-            def _():
-                reduce_a(g - 2)
-
-            @pl.when((pair == 1) & (g > 0))
-            def _():
-                merge(g - 1)
-                terms(g - 1)
-                swap(g - 1).start()
 
             attend_pair(g, pair)
 
@@ -412,7 +404,7 @@
         ref[last, 896:1024, :] = edge_ref[last % 2, 1, i].astype(BF16)
     for t in range(3):
         terms(last, (t,), t > 0)
-        swap_one(t).start()
+        swap(last, t).start()
     for r in range(2):
         rows = slice(r * 256, (r + 1) * 256)
         for n in range(4):
@@ -441,10 +433,10 @@
             gg_ref.at[:, n * 256:(n + 1) * 256], gg_hbm.at[:, n * 256:(n + 1) * 256], out_sem.at[1 + n]
         )
 
-    reduce_core_one(0)
-    reduce_core_one(1)
+    reduce_core(last, (0,))
+    reduce_core(last, (1,))
     merge(last)
-    reduce_core_one(2)
+    reduce_core(last, (2,))
     reduce_a(last - 1)
     grid_grads(0)
     grid_grads(1)
@@ -540,7 +532,7 @@
             dma((2, GROUPS)),
             dma((2, GROUPS, 2)),
             dma((2, GROUPS, 2)),
-            dma((2, GROUPS + 2)),
+            dma((2, GROUPS, 3)),
             dma((2, GROUPS)),
             dma((2, GROUPS)),
             dma((2, GROUPS)),

time: 78.3 us -> 77.7 us (level)
  no operation moved by 1% of the time
where the time goes in v6:
time: 77.7 us; the launch traced here: 77.6 us
  Pallas kernels  76.8 us (99%)
  between operations  0.8 us (1%)
    pallas_call x1, Pallas kernels, on_device(): pl.pallas_call(kernel, in_specs=[pl.BlockSpec(memory_space=pltpu.SMEM)] +...  73.9 us
    pallas_call x1, Pallas kernels, on_device(): pl.pallas_call(hand_out, in_specs=[anywhere] * 3, out_specs=[anywhere] *...  2.84 us

profile of v6, /device:TPU:0, one launch (start us, length us, event | category | flops | bytes accessed | tf_op | source)
XLA Modules:
  0.0 77.6 jit_solution(8807524911194927790)
XLA Ops:
  0.6 73.9 %shard_map.103 = (bf16[1024,1024]{1,0:T(8,128)(2,1)}, bf16[512,1024]{1,0:T(8,128)(2,1)}, f32[8,3072]{1,0:T(8,128)}) custom-call(s32[16]{0:T(128)} %ids_ref.1, bf16[1024,1024]{1,0:T(8,128)(2,1)} %bitcast.5, bf16[512,1024]{1,0:T(8,128)(2,1)} %bitcast.7, bf16[512,1024]{1,0:T(8,128)(2,1)} %bitcast.8, bf16[1024,1024]{1,0:T(8,128)(2,1)} %wq_hbm.1, ...), custom_call_target="tpu_custom_call" | custom-call | flops 21474836480 | bytes 20971520 | tf_op jit(solution)/shard_map/pallas_call | solution.py:482
  74.6 2.8 %shard_map.104 = (bf16[1024,1024]{1,0:T(8,128)(2,1)}, bf16[512,1024]{1,0:T(8,128)(2,1)}, f32[8,3072]{1,0:T(8,128)}) custom-call(bf16[1024,1024]{1,0:T(8,128)(2,1)} %get-tuple-element.9.gg, bf16[512,1024]{1,0:T(8,128)(2,1)} %get-tuple-element.10.mg, f32[8,3072]{1,0:T(8,128)} %get-tuple-element.11.wg), custom_call_target="tpu_custom_call" | custom-call | tf_op jit(solution)/shard_map/pallas_call | solution.py:546

commit v7 on v6

--- a/solution.py
+++ b/solution.py
@@ -242,9 +242,8 @@
             for side in range(2):
                 back(g, side).start()
 
-        @pl.loop(1, 7)
-        def _(block):
-            rows = pl.ds(pl.multiple_of(block * 128, 128), 128)
+        for block in range(1, 7):
+            rows = slice(block * 128, (block + 1) * 128)
             dk_ref[g, rows, cols] = gathered(dk_part, block + 1).astype(BF16)
             dv_ref[g, rows, cols] = gathered(dv_part, block + 1).astype(BF16)
 

time: 77.7 us -> 77.8 us (level)
  no operation moved by 1% of the time
where the time goes in v7:
time: 77.8 us; the launch traced here: 77.6 us
  Pallas kernels  76.8 us (99%)
  between operations  0.8 us (1%)
    pallas_call x1, Pallas kernels, on_device(): pl.pallas_call(kernel, in_specs=[pl.BlockSpec(memory_space=pltpu.SMEM)] +...  74 us
    pallas_call x1, Pallas kernels, on_device(): pl.pallas_call(hand_out, in_specs=[anywhere] * 3, out_specs=[anywhere] *...  2.84 us

profile of v7, /device:TPU:0, one launch (start us, length us, event | category | flops | bytes accessed | tf_op | source)
XLA Modules:
  0.0 77.6 jit_solution(1793875739909870056)
XLA Ops:
  0.6 74.0 %shard_map.103 = (bf16[1024,1024]{1,0:T(8,128)(2,1)}, bf16[512,1024]{1,0:T(8,128)(2,1)}, f32[8,3072]{1,0:T(8,128)}) custom-call(s32[16]{0:T(128)} %ids_ref.1, bf16[1024,1024]{1,0:T(8,128)(2,1)} %bitcast.5, bf16[512,1024]{1,0:T(8,128)(2,1)} %bitcast.7, bf16[512,1024]{1,0:T(8,128)(2,1)} %bitcast.8, bf16[1024,1024]{1,0:T(8,128)(2,1)} %wq_hbm.1, ...), custom_call_target="tpu_custom_call" | custom-call | flops 21474836480 | bytes 20971520 | tf_op jit(solution)/shard_map/pallas_call | solution.py:481
  74.6 2.8 %shard_map.104 = (bf16[1024,1024]{1,0:T(8,128)(2,1)}, bf16[512,1024]{1,0:T(8,128)(2,1)}, f32[8,3072]{1,0:T(8,128)}) custom-call(bf16[1024,1024]{1,0:T(8,128)(2,1)} %get-tuple-element.9.gg, bf16[512,1024]{1,0:T(8,128)(2,1)} %get-tuple-element.10.mg, f32[8,3072]{1,0:T(8,128)} %get-tuple-element.11.wg), custom_call_target="tpu_custom_call" | custom-call | tf_op jit(solution)/shard_map/pallas_call | solution.py:545
